TPU v7x, 256 devices: a whole 4x4x8 slice. The times are simulated.
256 devices in a mesh: expert: 8 (over z), tensor: 32 (over x, y, core).
Axes of the slice: x: 4, y: 4, z: 8, core: 2. Of those that a mesh axis runs over, the one named last changes fastest.
Arguments:
- tokens: bfloat16 [1024, 7168], P('expert', 'tensor'), may hold values from -48 to 48
- norm_gain: float32 [7168], replicated, may hold values from 0.25 to 1.75
- route_ids: int32 [1024, 2], P('expert'), may hold values from 0 to 7, all different within a row; in each aligned block of 128 rows (0 to 127, 128 to 255, ...) at most 48 rows name the same one
- route_probs: float32 [1024, 2], P('expert'), may hold values from 0.2 to 1
- dense_gate: bfloat16 [4864, 7168], P('tensor'), may hold values from -0.0625 to 0.0625
- dense_up: bfloat16 [4864, 7168], P('tensor'), may hold values from -0.0625 to 0.0625
- dense_down: bfloat16 [4864, 7168], P('tensor'), may hold values from -0.15625 to 0.15625
- expert_gate: bfloat16 [8, 4864, 7168], P('expert', 'tensor'), may hold values from -0.0625 to 0.0625
- expert_up: bfloat16 [8, 4864, 7168], P('expert', 'tensor'), may hold values from -0.0625 to 0.0625
- expert_down: bfloat16 [8, 4864, 7168], P('expert', 'tensor'), may hold values from -0.15625 to 0.15625
Outputs:
- block_out: bfloat16 [1024, 7168], P('expert', 'tensor')
Inputs may be any that keep to these rules, and one draw needn't show every extreme that they name: `route_ids`: in each aligned block of 128 rows (the rows of one index of the expert axis) no expert is named by more than 48 rows, a bound that some block reaches; the 2 ids of a row differ.
All inputs are finite; a program needn't handle non-finite values.
Results may differ from a plain program's by a relative error of at most 0.0064.
Values may be sent and summed in bfloat16 or wider, within the bound.
No kernel may reach another device: no remote copies, remote signals or barrier semaphores. Data moves between devices by JAX's collectives and lax.ppermute only.
A program may use at most 128 MiB of HBM per device.

v0:
```python
import jax
import jax.numpy as jnp
from jax import lax
from jax.sharding import PartitionSpec as P


def from_partner(x, axis, bit):
    return lax.ppermute(x, axis, [(i, i ^ 1 << bit) for i in range(lax.axis_size(axis))])


def row_product(left, weight_rows):
    return lax.dot_general(
        left, weight_rows, (((1,), (1,)), ((), ())), preferred_element_type=jnp.float32
    )


def shards(
    tokens,
    norm_gain,
    route_ids,
    route_probs,
    dense_gate,
    dense_up,
    dense_down,
    expert_gate,
    expert_up,
    expert_down,
):
    whole = lax.all_gather(tokens, "tensor", axis=1, tiled=True)
    values = whole.astype(jnp.float32)
    scale = lax.rsqrt(jnp.mean(values * values, axis=-1, keepdims=True) + 1e-05)
    normed = (values * scale * norm_gain).astype(jnp.bfloat16)
    experts = lax.axis_size("expert")
    tok_rows, choose = route_ids.shape
    capacity = 3 * tok_rows * choose // (2 * experts)
    feature_cols = tokens.shape[1]
    offset = lax.axis_index("tensor") * feature_cols
    own_index = lax.axis_index("expert")
    slot_expert = jnp.bitwise_xor(route_ids, own_index)
    flat_ids = route_ids.reshape(-1)
    onehot = (flat_ids[:, None] == jnp.arange(experts, dtype=jnp.int32)[None, :]).astype(jnp.int32)
    position = jnp.sum((jnp.cumsum(onehot, axis=0) - 1) * onehot, axis=1)
    slot_ids = (slot_expert.reshape(-1) * capacity + position).reshape(tok_rows, choose)
    slot_hits = (
        jnp.arange(experts * capacity, dtype=jnp.int32)[:, None, None] == slot_ids[None, :, :]
    )
    dispatch = jnp.any(slot_hits, axis=2).astype(jnp.bfloat16)
    combine = jnp.sum(jnp.where(slot_hits, route_probs[None, :, :], 0.0), axis=2)
    payload = lax.dynamic_slice_in_dim(normed, offset, feature_cols, 1)
    outgoing = jnp.dot(dispatch, payload, preferred_element_type=jnp.float32).astype(jnp.bfloat16)
    row_cols = outgoing.shape[1]
    blocks = outgoing.reshape(experts, capacity, row_cols)
    for level in range(experts.bit_length() - 1):
        stride = 1 << level
        paired = blocks.reshape(experts // (2 * stride), 2, stride, capacity, row_cols)
        arrived = from_partner(paired[:, 1], "expert", level)
        blocks = jnp.stack([paired[:, 0], arrived], axis=1).reshape(experts, capacity, row_cols)
    received = blocks.reshape(experts * capacity, row_cols)
    gate_proj = row_product(normed, dense_gate)
    up_proj = row_product(normed, dense_up)
    dense_hidden = (jax.nn.silu(gate_proj) * up_proj).astype(jnp.bfloat16)
    dense_partial = jnp.dot(dense_hidden, dense_down, preferred_element_type=jnp.float32)
    gate_weight = expert_gate[0]
    up_weight = expert_up[0]
    piece = lax.all_gather(received, "tensor", axis=1, tiled=True)
    expert_gates = row_product(piece, gate_weight)
    expert_ups = row_product(piece, up_weight)
    expert_hidden = (jax.nn.silu(expert_gates) * expert_ups).astype(jnp.bfloat16)
    partial_value = jnp.dot(expert_hidden, expert_down[0], preferred_element_type=jnp.float32)
    dense_share = lax.psum_scatter(dense_partial, "tensor", scatter_dimension=1, tiled=True)
    expert_share = lax.psum_scatter(partial_value, "tensor", scatter_dimension=1, tiled=True)
    result_cols = expert_share.shape[1]
    back = expert_share.reshape(experts, capacity, result_cols)
    for level in range(experts.bit_length() - 1):
        stride = 1 << level
        paired = back.reshape(experts // (2 * stride), 2, stride, capacity, result_cols)
        arrived = from_partner(paired[:, 1], "expert", level)
        back = jnp.stack([paired[:, 0], arrived], axis=1).reshape(experts, capacity, result_cols)
    returned = back.reshape(experts * capacity, result_cols)
    moe_out = jnp.dot(combine.T, returned, precision=lax.Precision.HIGHEST)
    total = dense_share + moe_out
    return total.astype(jnp.bfloat16)


def solution(mesh):
    in_specs = (
        P("expert", "tensor"),
        P(),
        P("expert", None),
        P("expert", None),
        P("tensor", None),
        P("tensor", None),
        P("tensor", None),
        P("expert", "tensor", None),
        P("expert", "tensor", None),
        P("expert", "tensor", None),
    )
    out_specs = P("expert", "tensor")
    return jax.shard_map(shards, mesh=mesh, in_specs=in_specs, out_specs=out_specs, check_vma=False)
```

profile of v0, /device:TPU:8, one launch (start us, length us, event | category | flops | bytes accessed | tf_op | source)
XLA Modules:
  0.0 364.3 jit_solution(4818674782647103654)
XLA Ops:
  6.5 0.0 copy-start
  6.5 0.0 copy-start.3
  6.5 0.0 all-gather.3.cloned.1.call-start
  6.5 0.7 all-gather.3.cloned.1.call-update
  7.3 0.0 all-gather.5.cloned.1.call-start
  7.3 0.8 copy.62
  8.1 0.1 eq.43
  8.2 0.1 eq.39
  8.4 0.6 reduce-window.6
  9.0 0.2 slice_reduce_fusion
  9.2 0.1 fusion.31
  9.3 0.1 reduce_sum.31
  9.5 0.1 copy.64
  9.5 0.7 multiply_add_fusion
  10.3 50.7 %all-gather.3.cloned.1.call-done = bf16[128,7168]{0,1:T(8,128)(2,1)} async-done(((bf16[128,224]{0,1:T(8,128)(2,1)}), bf16[128,7168]{0,1:T(8,128)(2,1)}) %all-gather.3.cloned.1.call-update) | async-done | bytes 1835024 | tf_op jit(solution)/shard_map/all_gather | solution.py:29
  61.0 0.0 copy-start.2
  61.0 2.6 fusion
  63.6 0.0 copy-done.3
  63.6 0.0 copy-done.2
  63.6 3.0 fusion.2
  66.6 0.0 copy-start.1
  66.6 1.2 copy-done.1
  67.8 0.2 convolution_convert_fusion
  68.0 0.1 copy.65
  68.2 1.6 collective-permute-start
  69.9 3.4 collective-permute-done
  73.3 2.6 collective-permute-start.1
  75.9 4.6 %collective-permute-done.1 = bf16[2,2,48,224]{3,2,0,1:T(8,128)(2,1)S(1)} collective-permute-done((bf16[2,2,48,224]{3,2,0,1:T(8,128)(2,1)S(1)}, bf16[2,2,48,224]{3,2,0,1:T(8,128)(2,1)S(1)}, u32[]{:S(2)}, u32[]{:S(2)}) %collective-permute-start.1) | collective-permute-done | bytes 86048 | tf_op jit(solution)/shard_map/ppermute | solution.py:8
  80.6 5.8 %collective-permute-start.2 = (bf16[1,4,48,224]{3,2,1,0:T(8,128)(2,1)S(1)}, bf16[1,4,48,224]{3,2,1,0:T(8,128)(2,1)S(1)}, u32[]{:S(2)}, u32[]{:S(2)}) collective-permute-start(bf16[1,4,48,224]{3,2,1,0:T(8,128)(2,1)S(1)} %get-tuple-element.12), channel_id=1, source_target_pairs={{0,128},{32,160},{64,192},{96,224},{128,0},{160,32},{192,64},{224,... | collective-permute-start | bytes 258056 | tf_op jit(solution)/shard_map/ppermute | solution.py:8
  86.5 2.8 collective-permute-done.2
  89.3 0.8 copy.69
  90.1 0.0 all-gather.5.cloned.1.call-update
  90.1 0.0 reduce-scatter.5.cloned.1.call-start
  90.2 52.9 %all-gather.5.cloned.1.call-done = bf16[384,7168]{0,1:T(8,128)(2,1)} async-done(((bf16[384,224]{0,1:T(8,128)(2,1)}), bf16[384,7168]{0,1:T(8,128)(2,1)}) %all-gather.5.cloned.1.call-update) | async-done | bytes 5505040 | tf_op jit(solution)/shard_map/all_gather | solution.py:65
  143.1 0.0 copy-start.5
  143.1 0.0 copy-start.6
  143.1 4.7 %fusion.7 = f32[384,152]{0,1:T(8,128)S(1)} fusion(bf16[384,7168]{0,1:T(8,128)(2,1)} %all-gather.5.cloned.1.call-done, bf16[1,152,7168]{2,1,0:T(8,128)(2,1)} %param.17), kind=kOutput, calls=%fused_computation.9 | convolution fusion | flops 836763648 | bytes 7917568 | tf_op jit(solution)/shard_map/dot_general | solution.py:12
  147.7 0.1 copy-done.5
  147.9 0.7 copy-done.6
  148.6 1.3 fusion.12
  149.9 0.0 copy-done
  149.9 6.4 %fusion.3 = f32[384,7168]{0,1:T(8,128)} fusion(bf16[384,152]{0,1:T(8,128)(2,1)S(1)} %fusion.12, bf16[1,152,7168]{2,1,0:T(8,128)(2,1)S(1)} %copy-done), kind=kOutput, calls=%fused_computation.5 | convolution fusion | flops 836763648 | bytes 13305856 | tf_op jit(solution)/shard_map/dot_general | solution.py:69
  156.2 0.0 reduce-scatter.5.cloned.1.call-update
  156.3 0.2 reduce-scatter.3.cloned.1.call-start
  156.5 2.9 fusion.39
  159.4 7.7 %fusion.17 = f32[128,7168]{0,1:T(8,128)} fusion(bf16[152,7168]{1,0:T(8,128)(2,1)} %param.16, bf16[128,7168]{0,1:T(8,128)(2,1)} %copy-done.1, bf16[152,7168]{1,0:T(8,128)(2,1)} %param.15, f32[128,152]{0,1:T(8,128)S(1)} %fusion.39), kind=kOutput, calls=%fused_computation.18 | convolution fusion | flops 557959168 | bytes 9940992 | tf_op jit(solution)/shard_map/dot_general | solution.py:62
  167.1 0.0 reduce-scatter.3.cloned.1.call-update
  167.1 0.0 copy-start.4
  167.1 95.9 %reduce-scatter.5.cloned.1.call-done = f32[384,224]{0,1:T(8,128)} async-done(((f32[384,7168]{0,1:T(8,128)}), f32[384,224]{0,1:T(8,128)}) %reduce-scatter.5.cloned.1.call-update) | async-done | bytes 344080 | tf_op jit(solution)/shard_map/reduce_scatter | solution.py:71
  263.0 1.1 copy.70
  264.2 1.6 collective-permute-start.3
  265.8 4.1 %collective-permute-done.3 = f32[4,1,48,224]{3,2,0,1:T(8,128)S(1)} collective-permute-done((f32[4,1,48,224]{3,2,0,1:T(8,128)S(1)}, f32[4,1,48,224]{3,2,0,1:T(8,128)S(1)}, u32[]{:S(2)}, u32[]{:S(2)}) %collective-permute-start.3) | collective-permute-done | bytes 172064 | tf_op jit(solution)/shard_map/ppermute | solution.py:8
  269.9 2.7 collective-permute-start.4
  272.6 7.0 %collective-permute-done.4 = f32[2,2,48,224]{3,2,0,1:T(8,128)S(1)} collective-permute-done((f32[2,2,48,224]{3,2,0,1:T(8,128)S(1)}, f32[2,2,48,224]{3,2,0,1:T(8,128)S(1)}, u32[]{:S(2)}, u32[]{:S(2)}) %collective-permute-start.4) | collective-permute-done | bytes 172064 | tf_op jit(solution)/shard_map/ppermute | solution.py:8
  279.7 5.9 %collective-permute-start.5 = (f32[1,4,48,224]{3,2,1,0:T(8,128)S(1)}, f32[1,4,48,224]{3,2,1,0:T(8,128)S(1)}, u32[]{:S(2)}, u32[]{:S(2)}) collective-permute-start(f32[1,4,48,224]{3,2,1,0:T(8,128)S(1)} %get-tuple-element.6), channel_id=1, source_target_pairs={{0,128},{32,160},{64,192},{96,224},{128,0},{160,32},{192,64},{224,... | collective-permute-start | bytes 516104 | tf_op jit(solution)/shard_map/ppermute | solution.py:8
  285.5 0.0 copy-done.4
  285.6 6.7 %collective-permute-done.5 = f32[1,4,48,224]{3,2,1,0:T(8,128)S(1)} collective-permute-done((f32[1,4,48,224]{3,2,1,0:T(8,128)S(1)}, f32[1,4,48,224]{3,2,1,0:T(8,128)S(1)}, u32[]{:S(2)}, u32[]{:S(2)}) %collective-permute-start.5) | collective-permute-done | bytes 172064 | tf_op jit(solution)/shard_map/ppermute | solution.py:8
  292.3 63.1 %reduce-scatter.3.cloned.1.call-done = f32[128,224]{0,1:T(8,128)} async-done(((f32[128,7168]{0,1:T(8,128)}), f32[128,224]{0,1:T(8,128)}) %reduce-scatter.3.cloned.1.call-update) | async-done | bytes 114704 | tf_op jit(solution)/shard_map/reduce_scatter | solution.py:70
  355.4 2.3 fusion.15
  (18 shorter events, 0.5 us)
Async XLA Ops:
  6.5 143.3 %copy-start = (bf16[1,152,7168]{2,1,0:T(8,128)(2,1)S(1)}, bf16[1,152,7168]{2,1,0:T(8,128)(2,1)}, u32[]{:S(2)}) copy-start(bf16[1,152,7168]{2,1,0:T(8,128)(2,1)} %param.19) | copy-start | bytes 6537220
  6.5 57.0 %copy-start.3 = (f32[7168]{0:T(1024)S(1)}, f32[7168]{0:T(1024)}, u32[]{:S(2)}) copy-start(f32[7168]{0:T(1024)} %param.11) | copy-start | bytes 86020
  6.5 54.4 %all-gather.3.cloned.1.call-start = ((), (), s32[]{:S(2)}) async-start(), calls=%async_computation.2 | async-start | bytes 1892352 | tf_op jit(solution)/shard_map/all_gather | solution.py:29
  7.3 135.8 %all-gather.5.cloned.1.call-start = ((), (), s32[]{:S(2)}) async-start(), calls=%async_computation.4 | async-start | bytes 5677056 | tf_op jit(solution)/shard_map/all_gather | solution.py:65
  61.0 2.6 copy-start.2
  66.6 1.2 copy-start.1
  68.2 5.1 %collective-permute-start = (bf16[4,1,48,224]{3,2,0,1:T(8,128)(2,1)S(1)}, bf16[4,1,48,224]{3,2,0,1:T(8,128)(2,1)S(1)}, u32[]{:S(2)}, u32[]{:S(2)}) collective-permute-start(bf16[4,1,48,224]{3,2,0,1:T(8,128)(2,1)S(1)} %get-tuple-element.16), channel_id=1, source_target_pairs={{0,32},{32,0},{64,96},{96,64},{128,160},{160,128},{192,224},{224,1... | collective-permute-start | bytes 258056 | tf_op jit(solution)/shard_map/ppermute | solution.py:8
  73.3 7.2 %collective-permute-start.1 = (bf16[2,2,48,224]{3,2,0,1:T(8,128)(2,1)S(1)}, bf16[2,2,48,224]{3,2,0,1:T(8,128)(2,1)S(1)}, u32[]{:S(2)}, u32[]{:S(2)}) collective-permute-start(bf16[2,2,48,224]{3,2,0,1:T(8,128)(2,1)S(1)} %get-tuple-element.14), channel_id=1, source_target_pairs={{0,64},{32,96},{64,0},{96,32},{128,192},{160,224},{192,128},{224,1... | collective-permute-start | bytes 258056 | tf_op jit(solution)/shard_map/ppermute | solution.py:8
  80.6 8.6 %collective-permute-start.2 = (bf16[1,4,48,224]{3,2,1,0:T(8,128)(2,1)S(1)}, bf16[1,4,48,224]{3,2,1,0:T(8,128)(2,1)S(1)}, u32[]{:S(2)}, u32[]{:S(2)}) collective-permute-start(bf16[1,4,48,224]{3,2,1,0:T(8,128)(2,1)S(1)} %get-tuple-element.12), channel_id=1, source_target_pairs={{0,128},{32,160},{64,192},{96,224},{128,0},{160,32},{192,64},{224,... | collective-permute-start | bytes 258056 | tf_op jit(solution)/shard_map/ppermute | solution.py:8
  90.1 172.8 %reduce-scatter.5.cloned.1.call-start = ((), (), s32[]{:S(2)}) async-start(), calls=%async_computation.5 | async-start | bytes 11354112 | tf_op jit(solution)/shard_map/reduce_scatter | solution.py:71
  143.1 4.8 %copy-start.5 = (bf16[384,7168]{0,1:T(8,128)(2,1)S(1)}, bf16[384,7168]{0,1:T(8,128)(2,1)}, u32[]{:S(2)}) copy-start(bf16[384,7168]{0,1:T(8,128)(2,1)} %all-gather.5.cloned.1.call-done) | copy-start | bytes 16515076
  143.1 5.5 %copy-start.6 = (bf16[1,152,7168]{2,1,0:T(8,128)(2,1)S(1)}, bf16[1,152,7168]{2,1,0:T(8,128)(2,1)}, u32[]{:S(2)}) copy-start(bf16[1,152,7168]{2,1,0:T(8,128)(2,1)} %param.18) | copy-start | bytes 6537220
  156.3 199.2 %reduce-scatter.3.cloned.1.call-start = ((), (), s32[]{:S(2)}) async-start(), calls=%async_computation.3 | async-start | bytes 3784704 | tf_op jit(solution)/shard_map/reduce_scatter | solution.py:70
  167.1 118.4 %copy-start.4 = (f32[128,2]{0,1:T(2,128)S(1)}, f32[128,2]{0,1:T(2,128)}, u32[]{:S(2)}) copy-start(f32[128,2]{0,1:T(2,128)} %param.13) | copy-start | bytes 3076
  264.2 5.8 %collective-permute-start.3 = (f32[4,1,48,224]{3,2,0,1:T(8,128)S(1)}, f32[4,1,48,224]{3,2,0,1:T(8,128)S(1)}, u32[]{:S(2)}, u32[]{:S(2)}) collective-permute-start(f32[4,1,48,224]{3,2,0,1:T(8,128)S(1)} %get-tuple-element.10), channel_id=1, source_target_pairs={{0,32},{32,0},{64,96},{96,64},{128,160},{160,128},{192,224},{224,1... | collective-permute-start | bytes 516104 | tf_op jit(solution)/shard_map/ppermute | solution.py:8
  269.9 9.6 %collective-permute-start.4 = (f32[2,2,48,224]{3,2,0,1:T(8,128)S(1)}, f32[2,2,48,224]{3,2,0,1:T(8,128)S(1)}, u32[]{:S(2)}, u32[]{:S(2)}) collective-permute-start(f32[2,2,48,224]{3,2,0,1:T(8,128)S(1)} %get-tuple-element.8), channel_id=1, source_target_pairs={{0,64},{32,96},{64,0},{96,32},{128,192},{160,224},{192,128},{224,1... | collective-permute-start | bytes 516104 | tf_op jit(solution)/shard_map/ppermute | solution.py:8
  279.7 12.6 %collective-permute-start.5 = (f32[1,4,48,224]{3,2,1,0:T(8,128)S(1)}, f32[1,4,48,224]{3,2,1,0:T(8,128)S(1)}, u32[]{:S(2)}, u32[]{:S(2)}) collective-permute-start(f32[1,4,48,224]{3,2,1,0:T(8,128)S(1)} %get-tuple-element.6), channel_id=1, source_target_pairs={{0,128},{32,160},{64,192},{96,224},{128,0},{160,32},{192,64},{224,... | collective-permute-start | bytes 516104 | tf_op jit(solution)/shard_map/ppermute | solution.py:8
Sparse Core Ops, SparseCore 0:
  9.9 51.0 all-gather.2
  90.3 52.7 all-gather.4
  156.4 106.5 reduce-scatter.4
  267.3 88.0 reduce-scatter.2
where the time goes:
time: 365 us; the launch traced here: 364 us
  waiting for transfers between devices  292 us (80%)
  matrix products  25.4 us (7%)
  starting transfers between devices  20.6 us (6%)
  between operations  13.3 us (4%)
  other arithmetic  7.31 us (2%)
  local copies, waits for them, and re-layouts  5.76 us (2%)
    reduce_scatter x1, waiting for transfers between devices, shards(): lax.psum_scatter(partial_value, 'tensor', scatter_dimension=1, tiled=True)  95.9 us
    reduce_scatter x1, waiting for transfers between devices, shards(): lax.psum_scatter(dense_partial, 'tensor', scatter_dimension=1, tiled=True)  63.1 us
    all_gather x1, waiting for transfers between devices, shards(): piece = lax.all_gather(received, 'tensor', axis=1, tiled=True)  52.9 us
    all_gather x1, waiting for transfers between devices, shards(): whole = lax.all_gather(tokens, 'tensor', axis=1, tiled=True)  50.7 us
    ppermute x6, waiting for transfers between devices, from_partner(): lax.ppermute(x, axis, [(i, i ^ 1 << bit) for i in range(lax.axis_size(axi...  28.6 us
    ppermute x6, starting transfers between devices, from_partner(): lax.ppermute(x, axis, [(i, i ^ 1 << bit) for i in range(lax.axis_size(axi...  20.2 us
    dot_general x3, matrix products, row_product(): lax.dot_general(left, weight_rows, (((1,), (1,)), ((), ())), preferred_el...  8.85 us
    dot_general x1, matrix products, shards(): jnp.dot(dense_hidden, dense_down, preferred_element_type=jnp.float32)  7.68 us
  transfers between devices with their start and end apart: 10, of which 10 were waited for; matrix products, arithmetic and copies ran while one was open for 4% of the time, Pallas kernels for 0%

commit v1 on v0

v1 whole, which is shorter than its diff:
```python
import functools

import jax
import jax.numpy as jnp
from jax import lax
from jax.experimental import pallas as pl
from jax.experimental.pallas import tpu as pltpu
from jax.sharding import PartitionSpec as P

SIDE = 4
PAIR = 2
CHIPS = SIDE * SIDE
VMEM = pltpu.MemorySpace.VMEM
SMEM = pltpu.MemorySpace.SMEM


def device_of(x, y, core):
    return (x * SIDE + y) * PAIR + core


def hops(step, first):
    pairs = []
    for x in range(SIDE):
        for y in range(SIDE):
            for core in range(PAIR):
                along_x = (core == 0) == first
                to_x = (x + step) % SIDE if along_x else x
                to_y = y if along_x else (y + step) % SIDE
                pairs.append((device_of(x, y, core), device_of(to_x, to_y, core)))
    return pairs


def sibling(value):
    return lax.ppermute(value, "tensor", [(i, i ^ 1) for i in range(CHIPS * PAIR)])


def chip_back(x, y, core, outer, inner):
    back_x = jnp.where(core == 0, inner, outer)
    back_y = jnp.where(core == 0, outer, inner)
    return lax.rem(x - back_x + SIDE, SIDE), lax.rem(y - back_y + SIDE, SIDE)


def hidden_kernel(dense_rows, place, *refs):
    stacks, refs = refs[: 2 * SIDE], refs[2 * SIDE :]
    gain, dense_gate, dense_up, expert_gate, expert_up, hidden, whole, arrived = refs
    x, y, core = place[0], place[1], place[2]
    cols = stacks[0].shape[1]
    width, rows = whole.shape
    copies = []
    for half in range(2):
        owner = core if half == 0 else 1 - core
        for outer in range(SIDE):
            for inner in range(SIDE):
                from_x, from_y = chip_back(x, y, owner, outer, inner)
                index = device_of(from_x, from_y, owner)
                copies.append(
                    pltpu.make_async_copy(
                        stacks[half * SIDE + outer].at[inner],
                        whole.at[pl.ds(pl.multiple_of(index * cols, 16), cols), :],
                        arrived.at[len(copies)],
                    )
                )
    for copy in copies:
        copy.start()
    for copy in copies:
        copy.wait()

    def squares(i, total):
        block = whole[pl.ds(pl.multiple_of(i * 32, 32), 32), :].astype(jnp.float32)
        block = block * block
        return total + jnp.sum(block.reshape(4, 8, rows), axis=0)

    total = lax.fori_loop(0, width // 32, squares, jnp.zeros((8, rows), jnp.float32), unroll=8)
    scale = lax.rsqrt(jnp.sum(total, axis=0, keepdims=True) / width + 1e-05)
    chunk = 896

    def product(weight, at, normed):
        return jnp.dot(weight[:, at], normed, preferred_element_type=jnp.float32)

    def step(k, sums):
        at = pl.ds(pl.multiple_of(k * chunk, chunk), chunk)
        gains = jnp.concatenate([gain[at, :]] * (rows // 128), axis=1)
        normed = (whole[at, :].astype(jnp.float32) * scale * gains).astype(jnp.bfloat16)
        dense, routed = normed[:, :dense_rows], normed[:, dense_rows:]
        return (
            sums[0] + product(dense_gate, at, dense),
            sums[1] + product(dense_up, at, dense),
            sums[2] + product(expert_gate, at, routed),
            sums[3] + product(expert_up, at, routed),
        )

    units = dense_gate.shape[0]
    zeros = lambda n: jnp.zeros((units, n), jnp.float32)
    sums = lax.fori_loop(
        0,
        width // chunk,
        step,
        (zeros(dense_rows), zeros(dense_rows), zeros(rows - dense_rows), zeros(rows - dense_rows)),
    )
    for gates, ups, span in (
        (sums[0], sums[1], slice(0, dense_rows)),
        (sums[2], sums[3], slice(dense_rows, rows)),
    ):
        hidden[:, span] = (gates / (1.0 + jnp.exp(-gates)) * ups).astype(jnp.bfloat16)


def hidden_units(place, stacks, gain, dense_gate, dense_up, expert_gate, expert_up, dense_rows):
    cols, rows = stacks[0].shape[1:]
    width = CHIPS * PAIR * cols
    in_vmem = pl.BlockSpec(memory_space=VMEM)
    return pl.pallas_call(
        functools.partial(hidden_kernel, dense_rows),
        out_shape=jax.ShapeDtypeStruct((dense_gate.shape[0], rows), jnp.bfloat16),
        in_specs=[pl.BlockSpec(memory_space=SMEM)]
        + [pl.BlockSpec(memory_space=pl.ANY)] * len(stacks)
        + [in_vmem] * 5,
        out_specs=in_vmem,
        scratch_shapes=[
            pltpu.VMEM((width, rows), jnp.bfloat16),
            pltpu.SemaphoreType.DMA((CHIPS * PAIR,)),
        ],
        compiler_params=pltpu.CompilerParams(vmem_limit_bytes=40 * 1024 * 1024),
        cost_estimate=pl.CostEstimate(
            flops=4 * dense_gate.shape[0] * rows * width, bytes_accessed=16 << 20, transcendentals=0
        ),
        name="hidden_units",
    )(place, *stacks, gain, dense_gate, dense_up, expert_gate, expert_up)


def down_kernel(dense_rows, place, hidden, *refs):
    for half in range(2):
        dense, routed, out = refs[2 * half], refs[2 * half + 1], refs[4 + half]
        for weight, span in (
            (dense, slice(0, dense_rows)),
            (routed, slice(dense_rows, hidden.shape[1])),
        ):
            out[0, :, span] = jnp.dot(
                weight[...], hidden[:, span], preferred_element_type=jnp.float32
            ).astype(jnp.bfloat16)


def down_pieces(place, hidden, dense_down, expert_down, outer, cols, dense_rows):
    units, rows = hidden.shape

    def block(half):
        def index(inner, place):
            x, y, core = place[0], place[1], place[2]
            owner = core if half == 0 else 1 - core
            to_x = lax.rem(x + jnp.where(owner == 0, inner, outer), SIDE)
            to_y = lax.rem(y + jnp.where(owner == 0, outer, inner), SIDE)
            return device_of(to_x, to_y, owner), 0

        return pl.BlockSpec((cols, units), index)

    out = pl.BlockSpec((1, cols, rows), lambda inner, place: (inner, 0, 0))
    shape = jax.ShapeDtypeStruct((SIDE, cols, rows), jnp.bfloat16)
    return pl.pallas_call(
        functools.partial(down_kernel, dense_rows),
        out_shape=(shape, shape),
        grid_spec=pltpu.PrefetchScalarGridSpec(
            num_scalar_prefetch=1,
            grid=(SIDE,),
            in_specs=[
                pl.BlockSpec((units, rows), lambda inner, place: (0, 0)),
                block(0),
                block(0),
                block(1),
                block(1),
            ],
            out_specs=(out, out),
        ),
        compiler_params=pltpu.CompilerParams(vmem_limit_bytes=16 * 1024 * 1024),
        cost_estimate=pl.CostEstimate(
            flops=4 * SIDE * cols * rows * units, bytes_accessed=4 << 20, transcendentals=0
        ),
        name=f"down_pieces_{outer}",
    )(place, hidden, dense_down, expert_down, dense_down, expert_down)


def shards(
    tokens,
    norm_gain,
    route_ids,
    route_probs,
    dense_gate,
    dense_up,
    dense_down,
    expert_gate,
    expert_up,
    expert_down,
):
    f32, bf16 = jnp.float32, jnp.bfloat16
    experts = lax.axis_size("expert")
    tok_rows, choose = route_ids.shape
    cols = tokens.shape[1]
    capacity = 3 * tok_rows * choose // (2 * experts)
    index = lax.axis_index("tensor")
    core = index % PAIR
    place = jnp.stack([index // (SIDE * PAIR), index // PAIR % SIDE, core]).astype(jnp.int32)

    flat_ids = route_ids.reshape(-1)
    onehot = (flat_ids[:, None] == jnp.arange(experts, dtype=jnp.int32)[None, :]).astype(jnp.int32)
    position = jnp.sum((jnp.cumsum(onehot, axis=0) - 1) * onehot, axis=1)
    slot_ids = (flat_ids * capacity + position).reshape(tok_rows, choose)
    slot_hits = (
        jnp.arange(experts * capacity, dtype=jnp.int32)[:, None, None] == slot_ids[None, :, :]
    )
    dispatch = jnp.any(slot_hits, axis=2).astype(bf16)
    combine = jnp.sum(jnp.where(slot_hits, route_probs[None, :, :], 0.0), axis=2)

    outgoing = jnp.dot(dispatch, tokens, preferred_element_type=f32).astype(bf16)
    received = lax.all_to_all(
        outgoing.reshape(experts, capacity, cols), "expert", 0, 0, tiled=True
    ).reshape(experts * capacity, cols)
    own = jnp.concatenate([tokens.T, received.T], axis=1)

    first = [own] + [lax.ppermute(own, "tensor", hops(d, True)) for d in range(1, SIDE)]
    stack = jnp.stack(first)
    stacks = [stack] + [lax.ppermute(stack, "tensor", hops(d, False)) for d in range(1, SIDE)]
    others = [sibling(part) for part in stacks]

    gain = jnp.broadcast_to(norm_gain[:, None], (norm_gain.shape[0], 128))
    hidden = hidden_units(
        place, stacks + others, gain, dense_gate, dense_up, expert_gate[0], expert_up[0], tok_rows
    )

    dense_down, routed_down = dense_down.T, expert_down[0].T
    pieces = {}
    for outer in (1, 2, 3, 0):
        mine, others = down_pieces(place, hidden, dense_down, routed_down, outer, cols, tok_rows)
        pieces[outer] = mine.astype(f32) + sibling(others).astype(f32)
    level = pieces[0]
    for d in range(1, SIDE):
        level = level + lax.ppermute(pieces[d].astype(bf16), "tensor", hops(d, False)).astype(f32)
    total = level[0]
    for d in range(1, SIDE):
        total = total + lax.ppermute(level[d].astype(bf16), "tensor", hops(d, True)).astype(f32)

    back = total[:, tok_rows:].T.reshape(experts, capacity, cols)
    returned = lax.all_to_all(back, "expert", 0, 0, tiled=True).reshape(experts * capacity, cols)
    moe_out = jnp.dot(combine.T, returned, precision=lax.Precision.HIGHEST)
    return (total[:, :tok_rows].T + moe_out).astype(bf16)


def solution(mesh):
    in_specs = (
        P("expert", "tensor"),
        P(),
        P("expert", None),
        P("expert", None),
        P("tensor", None),
        P("tensor", None),
        P("tensor", None),
        P("expert", "tensor", None),
        P("expert", "tensor", None),
        P("expert", "tensor", None),
    )
    out_specs = P("expert", "tensor")
    return jax.shard_map(shards, mesh=mesh, in_specs=in_specs, out_specs=out_specs, check_vma=False)
```

time: 365 us -> 156 us (0.43)
  waiting for transfers between devices: 292 us -> 60.4 us
  matrix products: 25.4 us -> 2.46 us
  Pallas kernels: 0 us -> 22.4 us
  blocking collectives: 0 us -> 18.9 us
  between operations: 13.3 us -> 0.26 us
  local copies, waits for them, and re-layouts: 5.76 us -> 16.3 us
  starting transfers between devices: 20.6 us -> 30.4 us
  other arithmetic: 7.31 us -> 3.41 us
    reduce_scatter x2 -> x0, waiting for transfers between devices: 159 us -> none  [the longest x1 95.9 us: shards(): lax.psum_scatter(partial_value, 'tensor', scatter_dimension=1, tiled=True)]
    all_gather x2 -> x0, waiting for transfers between devices: 104 us -> none  [the longest x1 52.9 us: shards(): piece = lax.all_gather(received, 'tensor', axis=1, tiled=True)]
    pallas_call x0 -> x5, Pallas kernels: none -> 22.4 us  [the longest x1 14.9 us: hidden_units(): pl.pallas_call(functools.partial(hidden_kernel, dense_rows), out_shape=ja...]
    dot_general x6 -> x1, matrix products: 23.1 us -> 1.04 us  [shards(): jnp.dot(dispatch, tokens, preferred_element_type=f32).astype(bf16)]
    ppermute x6 -> x20, waiting for transfers between devices: 28.6 us -> 47.7 us  [the longest x3 21.4 us: shards(): lax.ppermute(pieces[d].astype(bf16), 'tensor', hops(d, False)).astype(f32)]
    all_to_all x0 -> x1, blocking collectives: none -> 18.9 us  [shards(): lax.all_to_all(outgoing.reshape(experts, capacity, cols), 'expert', 0, 0,...]
    all_to_all x0 -> x1, waiting for transfers between devices: none -> 12.8 us  [shards(): lax.all_to_all(back, 'expert', 0, 0, tiled=True)]
    unnamed x15 -> x21, local copies, waits for them, and re-layouts: 2.85 us -> 10.2 us
  transfers between devices with their start and end apart: 10 -> 21, of which waited for: 10 -> 12; matrix products, arithmetic and copies ran while one was open for 4% -> 6% of each run, Pallas kernels for 0% -> 4%
where the time goes in v1:
time: 156 us; the launch traced here: 155 us
  waiting for transfers between devices  60.4 us (39%)
  starting transfers between devices  30.4 us (19%)
  Pallas kernels  22.4 us (14%)
  blocking collectives  18.9 us (12%)
  local copies, waits for them, and re-layouts  16.3 us (10%)
  other arithmetic  3.41 us (2%)
  matrix products  2.46 us (2%)
    ppermute x3, waiting for transfers between devices, shards(): lax.ppermute(pieces[d].astype(bf16), 'tensor', hops(d, False)).astype(f32)  21.4 us
    all_to_all x1, blocking collectives, shards(): lax.all_to_all(outgoing.reshape(experts, capacity, cols), 'expert', 0, 0,...  18.9 us
    ppermute x3, waiting for transfers between devices, shards(): lax.ppermute(stack, 'tensor', hops(d, False))  16.3 us
    pallas_call x1, Pallas kernels, hidden_units(): pl.pallas_call(functools.partial(hidden_kernel, dense_rows), out_shape=ja...  14.9 us
    all_to_all x1, waiting for transfers between devices, shards(): lax.all_to_all(back, 'expert', 0, 0, tiled=True)  12.8 us
    unnamed x21, local copies, waits for them, and re-layouts  10.2 us
    pallas_call x4, Pallas kernels, down_pieces(): pl.pallas_call(functools.partial(down_kernel, dense_rows), out_shape=(sha...  7.52 us
    ppermute x8, starting transfers between devices, sibling(): lax.ppermute(value, 'tensor', [(i, i ^ 1) for i in range(CHIPS * PAIR)])  6.22 us
  transfers between devices with their start and end apart: 21, of which 12 were waited for; matrix products, arithmetic and copies ran while one was open for 6% of the time, Pallas kernels for 4%

profile of v1, /device:TPU:8, one launch (start us, length us, event | category | flops | bytes accessed | tf_op | source)
XLA Modules:
  0.0 154.6 jit_solution(6266439266435080271)
XLA Ops:
  0.0 0.8 copy.35
  0.8 0.1 eq.46
  0.9 0.1 eq.42
  1.1 0.6 reduce-window.6
  1.7 0.2 slice_reduce_fusion
  1.9 0.1 fusion.6
  2.0 0.1 reduce_sum.21
  2.2 0.1 copy.37
  2.2 0.7 multiply_add_fusion
  3.0 1.0 convolution_convert_fusion
  4.0 0.0 copy-start.5
  4.1 0.1 copy.38
  4.2 18.9 %all_to_all.10 = bf16[8,48,224]{2,1,0:T(8,128)(2,1)S(1)} all-to-all(bf16[8,48,224]{2,1,0:T(8,128)(2,1)S(1)} %bitcast.71), channel_id=1, replica_groups=mesh['expert'=8,'tensor'=32] {'expert'}, dimensions={0} | all-to-all | bytes 344064 | tf_op jit(solution)/shard_map/all_to_all | solution.py:212
  23.1 0.1 copy.39
  23.3 1.6 %collective-permute-start = (bf16[224,512]{1,0:T(8,128)(2,1)S(1)}, bf16[224,512]{1,0:T(8,128)(2,1)S(1)}, u32[]{:S(2)}, u32[]{:S(2)}) collective-permute-start(bf16[224,512]{1,0:T(8,128)(2,1)S(1)} %get-tuple-element.27), channel_id=1, source_target_pairs={{0,8},{1,3},{2,10},{3,5},{4,12},{5,7},{6,14},{7,1},{8,16},{9,11},{... | collective-permute-start | bytes 688136 | tf_op jit(solution)/shard_map/ppermute | solution.py:217
  24.8 2.7 %collective-permute-start.1 = (bf16[224,512]{1,0:T(8,128)(2,1)S(1)}, bf16[224,512]{1,0:T(8,128)(2,1)S(1)}, u32[]{:S(2)}, u32[]{:S(2)}) collective-permute-start(bf16[224,512]{1,0:T(8,128)(2,1)S(1)} %get-tuple-element.27), channel_id=1, source_target_pairs={{0,16},{1,5},{2,18},{3,7},{4,20},{5,1},{6,22},{7,3},{8,24},{9,13},... | collective-permute-start | bytes 688136 | tf_op jit(solution)/shard_map/ppermute | solution.py:217
  27.6 1.4 collective-permute-start.2
  29.0 1.6 %collective-permute-done = bf16[224,512]{1,0:T(8,128)(2,1)S(1)} collective-permute-done((bf16[224,512]{1,0:T(8,128)(2,1)S(1)}, bf16[224,512]{1,0:T(8,128)(2,1)S(1)}, u32[]{:S(2)}, u32[]{:S(2)}) %collective-permute-start) | collective-permute-done | bytes 229408 | tf_op jit(solution)/shard_map/ppermute | solution.py:217
  30.6 3.4 %collective-permute-done.1 = bf16[224,512]{1,0:T(8,128)(2,1)S(1)} collective-permute-done((bf16[224,512]{1,0:T(8,128)(2,1)S(1)}, bf16[224,512]{1,0:T(8,128)(2,1)S(1)}, u32[]{:S(2)}, u32[]{:S(2)}) %collective-permute-start.1) | collective-permute-done | bytes 229408 | tf_op jit(solution)/shard_map/ppermute | solution.py:217
  34.0 0.0 collective-permute-done.2
  34.0 0.1 pad_maximum_fusion.refs_0_
  34.2 1.7 %collective-permute-start.3 = (bf16[4,224,512]{2,1,0:T(8,128)(2,1)S(1)}, bf16[4,224,512]{2,1,0:T(8,128)(2,1)}, u32[]{:S(2)}, u32[]{:S(2)}) collective-permute-start(bf16[4,224,512]{2,1,0:T(8,128)(2,1)S(1)} %pad_maximum_fusion.refs_0_), channel_id=1, source_target_pairs={{0,2},{1,9},{2,4},{3,11},{4,6},{5,13},{6,0},{7,15},{8,10},{9,17},{... | collective-permute-start | bytes 2752520 | tf_op jit(solution)/shard_map/ppermute | solution.py:219
  35.8 0.9 collective-permute-start.4
  36.7 2.4 %collective-permute-start.5 = (bf16[4,224,512]{2,1,0:T(8,128)(2,1)S(1)}, bf16[4,224,512]{2,1,0:T(8,128)(2,1)}, u32[]{:S(2)}, u32[]{:S(2)}) collective-permute-start(bf16[4,224,512]{2,1,0:T(8,128)(2,1)S(1)} %pad_maximum_fusion.refs_0_), channel_id=1, source_target_pairs={{0,6},{1,25},{2,0},{3,27},{4,2},{5,29},{6,4},{7,31},{8,14},{9,1},{... | collective-permute-start | bytes 2752520 | tf_op jit(solution)/shard_map/ppermute | solution.py:219
  39.2 8.6 %collective-permute-done.3.refs_1_ = bf16[4,224,512]{2,1,0:T(8,128)(2,1)} collective-permute-done((bf16[4,224,512]{2,1,0:T(8,128)(2,1)S(1)}, bf16[4,224,512]{2,1,0:T(8,128)(2,1)}, u32[]{:S(2)}, u32[]{:S(2)}) %collective-permute-start.3) | collective-permute-done | bytes 917536 | tf_op jit(solution)/shard_map/ppermute | solution.py:219
  47.7 0.0 collective-permute-start.7
  47.7 3.2 %collective-permute-done.4.refs_2_ = bf16[4,224,512]{2,1,0:T(8,128)(2,1)} collective-permute-done((bf16[4,224,512]{2,1,0:T(8,128)(2,1)S(1)}, bf16[4,224,512]{2,1,0:T(8,128)(2,1)}, u32[]{:S(2)}, u32[]{:S(2)}) %collective-permute-start.4) | collective-permute-done | bytes 917536 | tf_op jit(solution)/shard_map/ppermute | solution.py:219
  50.9 4.7 %collective-permute-start.8 = (bf16[4,224,512]{2,1,0:T(8,128)(2,1)}, bf16[4,224,512]{2,1,0:T(8,128)(2,1)}, u32[]{:S(2)}, u32[]{:S(2)}) collective-permute-start(bf16[4,224,512]{2,1,0:T(8,128)(2,1)} %collective-permute-done.4.refs_2_), channel_id=1, source_target_pairs={{0,1},{1,0},{2,3},{3,2},{4,5},{5,4},{6,7},{7,6},{8,9},{9,8},{10,11... | collective-permute-start | bytes 2752520 | tf_op jit(solution)/shard_map/ppermute | solution.py:34
  55.6 4.5 %collective-permute-done.5.refs_3_ = bf16[4,224,512]{2,1,0:T(8,128)(2,1)} collective-permute-done((bf16[4,224,512]{2,1,0:T(8,128)(2,1)S(1)}, bf16[4,224,512]{2,1,0:T(8,128)(2,1)}, u32[]{:S(2)}, u32[]{:S(2)}) %collective-permute-start.5) | collective-permute-done | bytes 917536 | tf_op jit(solution)/shard_map/ppermute | solution.py:219
  60.1 3.0 %copy.40 = bf16[152,7168]{0,1:T(8,128)(2,1)} copy(bf16[152,7168]{1,0:T(8,128)(2,1)S(1)} %copy-done.5) | data formatting | bytes 4358144 | tf_op args[6]
  63.0 4.8 %copy.41 = bf16[1,152,7168]{1,2,0:T(8,128)(2,1)} copy(bf16[1,152,7168]{2,1,0:T(8,128)(2,1)} %param.19) | data formatting | bytes 4358144 | tf_op args[9]
  67.8 0.1 pad_add_fusion.place
  67.9 4.2 %broadcast_in_dim.14.refs_8_ = f32[7168,128]{1,0:T(8,128)} broadcast(f32[7168]{0:T(1024)S(1)} %copy-done.7), dimensions={0} | broadcast | bytes 3698688 | tf_op jit(solution)/shard_map/broadcast_in_dim | solution.py:222
  72.1 1.6 %copy-done.4 = bf16[1,152,7168]{2,1,0:T(8,128)(2,1)S(1)} copy-done((bf16[1,152,7168]{2,1,0:T(8,128)(2,1)S(1)}, bf16[1,152,7168]{2,1,0:T(8,128)(2,1)}, u32[]{:S(2)}) %copy-start.4) | copy-done | bytes 2179096
  73.7 14.9 %hidden_units.1.hidden = bf16[152,512]{1,0:T(8,128)(2,1)S(1)} custom-call(s32[3]{0:T(128)S(1)} %pad_add_fusion.place, bf16[4,224,512]{2,1,0:T(8,128)(2,1)S(1)} %pad_maximum_fusion.refs_0_, bf16[4,224,512]{2,1,0:T(8,128)(2,1)} %collective-permute-done.3.refs_1_, bf16[4,224,512]{2,1,0:T(8,128)(2,1)} %collective-permute-done.4.refs_2_, ...), custom_call_target="tpu_custom_call" | custom-call | flops 2231369728 | bytes 16777216 | tf_op jit(solution)/shard_map/hidden_units/pallas_call | solution.py:111
  88.7 1.9 %down_pieces_1.1 = (bf16[4,224,512]{2,1,0:T(8,128)(2,1)S(1)}, bf16[4,224,512]{2,1,0:T(8,128)(2,1)S(1)}) custom-call(s32[3]{0:T(128)S(1)} %pad_add_fusion.place, bf16[152,512]{1,0:T(8,128)(2,1)S(1)} %hidden_units.1.hidden, bf16[7168,152]{1,0:T(8,128)(2,1)S(1)} %bitcast.52, bf16[7168,152]{1,0:T(8,128)(2,1)S(1)} %bitcast.60, bf16[7168,152]{1,0:T(8,128)(2,1)S(1)} %bitcast.53, ...), custom_call_target="tpu_custom_call" | custom-call | flops 278921216 | bytes 4194304 | tf_op jit(solution)/shard_map/down_pieces_1/pallas_call | solution.py:157
  90.6 0.8 collective-permute-start.11
  91.3 1.9 %down_pieces_2.1 = (bf16[4,224,512]{2,1,0:T(8,128)(2,1)S(1)}, bf16[4,224,512]{2,1,0:T(8,128)(2,1)S(1)}) custom-call(s32[3]{0:T(128)S(1)} %pad_add_fusion.place, bf16[152,512]{1,0:T(8,128)(2,1)S(1)} %hidden_units.1.hidden, bf16[7168,152]{1,0:T(8,128)(2,1)S(1)} %bitcast.54, bf16[7168,152]{1,0:T(8,128)(2,1)S(1)} %bitcast.62, bf16[7168,152]{1,0:T(8,128)(2,1)S(1)} %bitcast.55, ...), custom_call_target="tpu_custom_call" | custom-call | flops 278921216 | bytes 4194304 | tf_op jit(solution)/shard_map/down_pieces_2/pallas_call | solution.py:157
  93.2 0.1 collective-permute-start.13
  93.3 1.9 %down_pieces_3.1 = (bf16[4,224,512]{2,1,0:T(8,128)(2,1)S(1)}, bf16[4,224,512]{2,1,0:T(8,128)(2,1)S(1)}) custom-call(s32[3]{0:T(128)S(1)} %pad_add_fusion.place, bf16[152,512]{1,0:T(8,128)(2,1)S(1)} %hidden_units.1.hidden, bf16[7168,152]{1,0:T(8,128)(2,1)S(1)} %bitcast.56, bf16[7168,152]{1,0:T(8,128)(2,1)S(1)} %bitcast.64, bf16[7168,152]{1,0:T(8,128)(2,1)S(1)} %bitcast.57, ...), custom_call_target="tpu_custom_call" | custom-call | flops 278921216 | bytes 4194304 | tf_op jit(solution)/shard_map/down_pieces_3/pallas_call | solution.py:157
  95.2 0.6 collective-permute-start.15
  95.8 1.9 %down_pieces_0.1 = (bf16[4,224,512]{2,1,0:T(8,128)(2,1)S(1)}, bf16[4,224,512]{2,1,0:T(8,128)(2,1)S(1)}) custom-call(s32[3]{0:T(128)S(1)} %pad_add_fusion.place, bf16[152,512]{1,0:T(8,128)(2,1)S(1)} %hidden_units.1.hidden, bf16[7168,152]{1,0:T(8,128)(2,1)S(1)} %bitcast.58, bf16[7168,152]{1,0:T(8,128)(2,1)S(1)} %bitcast.66, bf16[7168,152]{1,0:T(8,128)(2,1)S(1)} %bitcast.59, ...), custom_call_target="tpu_custom_call" | custom-call | flops 278921216 | bytes 4194304 | tf_op jit(solution)/shard_map/down_pieces_0/pallas_call | solution.py:157
  97.7 0.1 collective-permute-start.10
  97.8 0.3 add_convert_fusion.2
  98.1 1.3 collective-permute-start.12
  99.3 0.3 add_convert_fusion.1
  99.6 1.9 %collective-permute-start.14 = (bf16[4,224,512]{2,1,0:T(8,128)(2,1)S(1)}, bf16[4,224,512]{2,1,0:T(8,128)(2,1)S(1)}, u32[]{:S(2)}, u32[]{:S(2)}) collective-permute-start(bf16[4,224,512]{2,1,0:T(8,128)(2,1)S(1)} %add_convert_fusion.1), channel_id=1, source_target_pairs={{0,4},{1,17},{2,6},{3,19},{4,0},{5,21},{6,2},{7,23},{8,12},{9,25},... | collective-permute-start | bytes 2752520 | tf_op jit(solution)/shard_map/ppermute | solution.py:234
  101.5 0.3 add_convert_fusion
  101.8 1.3 collective-permute-start.16
  103.0 8.5 %collective-permute-done.12 = bf16[4,224,512]{2,1,0:T(8,128)(2,1)S(1)} collective-permute-done((bf16[4,224,512]{2,1,0:T(8,128)(2,1)S(1)}, bf16[4,224,512]{2,1,0:T(8,128)(2,1)S(1)}, u32[]{:S(2)}, u32[]{:S(2)}) %collective-permute-start.12) | collective-permute-done | bytes 917536 | tf_op jit(solution)/shard_map/ppermute | solution.py:234
  111.5 3.2 %collective-permute-done.14 = bf16[4,224,512]{2,1,0:T(8,128)(2,1)S(1)} collective-permute-done((bf16[4,224,512]{2,1,0:T(8,128)(2,1)S(1)}, bf16[4,224,512]{2,1,0:T(8,128)(2,1)S(1)}, u32[]{:S(2)}, u32[]{:S(2)}) %collective-permute-start.14) | collective-permute-done | bytes 917536 | tf_op jit(solution)/shard_map/ppermute | solution.py:234
  114.7 9.7 %collective-permute-done.16 = bf16[4,224,512]{2,1,0:T(8,128)(2,1)S(1)} collective-permute-done((bf16[4,224,512]{2,1,0:T(8,128)(2,1)S(1)}, bf16[4,224,512]{2,1,0:T(8,128)(2,1)S(1)}, u32[]{:S(2)}, u32[]{:S(2)}) %collective-permute-start.16) | collective-permute-done | bytes 917536 | tf_op jit(solution)/shard_map/ppermute | solution.py:234
  124.4 0.7 fusion.9
  125.2 2.0 %collective-permute-start.17 = (bf16[224,512]{1,0:T(8,128)(2,1)S(1)}, bf16[224,512]{1,0:T(8,128)(2,1)S(1)}, u32[]{:S(2)}, u32[]{:S(2)}) collective-permute-start(bf16[224,512]{1,0:T(8,128)(2,1)S(1)} %get-tuple-element.23), channel_id=1, source_target_pairs={{0,8},{1,3},{2,10},{3,5},{4,12},{5,7},{6,14},{7,1},{8,16},{9,11},{... | collective-permute-start | bytes 688136 | tf_op jit(solution)/shard_map/ppermute | solution.py:237
  127.2 2.1 %collective-permute-start.18 = (bf16[224,512]{1,0:T(8,128)(2,1)S(1)}, bf16[224,512]{1,0:T(8,128)(2,1)S(1)}, u32[]{:S(2)}, u32[]{:S(2)}) collective-permute-start(bf16[224,512]{1,0:T(8,128)(2,1)S(1)} %get-tuple-element.25), channel_id=1, source_target_pairs={{0,16},{1,5},{2,18},{3,7},{4,20},{5,1},{6,22},{7,3},{8,24},{9,13},... | collective-permute-start | bytes 688136 | tf_op jit(solution)/shard_map/ppermute | solution.py:237
  129.3 1.6 %collective-permute-start.19 = (bf16[224,512]{1,0:T(8,128)(2,1)S(1)}, bf16[224,512]{1,0:T(8,128)(2,1)S(1)}, u32[]{:S(2)}, u32[]{:S(2)}) collective-permute-start(bf16[224,512]{1,0:T(8,128)(2,1)S(1)} %get-tuple-element.24), channel_id=1, source_target_pairs={{0,24},{1,7},{2,26},{3,1},{4,28},{5,3},{6,30},{7,5},{8,0},{9,15},{... | collective-permute-start | bytes 688136 | tf_op jit(solution)/shard_map/ppermute | solution.py:237
  130.8 1.7 %collective-permute-done.17 = bf16[224,512]{1,0:T(8,128)(2,1)S(1)} collective-permute-done((bf16[224,512]{1,0:T(8,128)(2,1)S(1)}, bf16[224,512]{1,0:T(8,128)(2,1)S(1)}, u32[]{:S(2)}, u32[]{:S(2)}) %collective-permute-start.17) | collective-permute-done | bytes 229408 | tf_op jit(solution)/shard_map/ppermute | solution.py:237
  132.5 3.2 %collective-permute-done.18 = bf16[224,512]{1,0:T(8,128)(2,1)S(1)} collective-permute-done((bf16[224,512]{1,0:T(8,128)(2,1)S(1)}, bf16[224,512]{1,0:T(8,128)(2,1)S(1)}, u32[]{:S(2)}, u32[]{:S(2)}) %collective-permute-start.18) | collective-permute-done | bytes 229408 | tf_op jit(solution)/shard_map/ppermute | solution.py:237
  135.7 0.1 collective-permute-done.19
  135.8 0.1 fusion.2
  136.0 0.9 copy.42
  136.9 3.5 %all-to-all-start.1 = ((f32[8,48,224]{2,1,0:T(8,128)}), f32[8,48,224]{2,1,0:T(8,128)S(1)}, u32[]{:S(2)}, u32[]{:S(2)}) async-start(f32[8,48,224]{2,1,0:T(8,128)} %bitcast.25), calls=%async_computation.1 | async-start | bytes 786432 | tf_op jit(solution)/shard_map/all_to_all | solution.py:240
  140.4 12.8 %all-to-all-done.1 = f32[8,48,224]{2,1,0:T(8,128)S(1)} async-done(((f32[8,48,224]{2,1,0:T(8,128)}), f32[8,48,224]{2,1,0:T(8,128)S(1)}, u32[]{:S(2)}, u32[]{:S(2)}) %all-to-all-start.1) | async-done | bytes 344096 | tf_op jit(solution)/shard_map/all_to_all | solution.py:240
  153.2 1.4 fusion.5
  (34 shorter events, 0.3 us)
Async XLA Ops:
  0.0 23.2 %copy-start.6 = (bf16[128,224]{0,1:T(8,128)(2,1)S(1)}, bf16[128,224]{0,1:T(8,128)(2,1)}, u32[]{:S(2)}) copy-start(bf16[128,224]{0,1:T(8,128)(2,1)} %param.10) | copy-start | bytes 172036
  4.0 56.0 %copy-start.5 = (bf16[152,7168]{1,0:T(8,128)(2,1)S(1)}, bf16[152,7168]{1,0:T(8,128)(2,1)}, u32[]{:S(2)}) copy-start(bf16[152,7168]{1,0:T(8,128)(2,1)} %param.16) | copy-start | bytes 6537220
  23.3 7.3 %collective-permute-start = (bf16[224,512]{1,0:T(8,128)(2,1)S(1)}, bf16[224,512]{1,0:T(8,128)(2,1)S(1)}, u32[]{:S(2)}, u32[]{:S(2)}) collective-permute-start(bf16[224,512]{1,0:T(8,128)(2,1)S(1)} %get-tuple-element.27), channel_id=1, source_target_pairs={{0,8},{1,3},{2,10},{3,5},{4,12},{5,7},{6,14},{7,1},{8,16},{9,11},{... | collective-permute-start | bytes 688136 | tf_op jit(solution)/shard_map/ppermute | solution.py:217
  24.8 9.2 %collective-permute-start.1 = (bf16[224,512]{1,0:T(8,128)(2,1)S(1)}, bf16[224,512]{1,0:T(8,128)(2,1)S(1)}, u32[]{:S(2)}, u32[]{:S(2)}) collective-permute-start(bf16[224,512]{1,0:T(8,128)(2,1)S(1)} %get-tuple-element.27), channel_id=1, source_target_pairs={{0,16},{1,5},{2,18},{3,7},{4,20},{5,1},{6,22},{7,3},{8,24},{9,13},... | collective-permute-start | bytes 688136 | tf_op jit(solution)/shard_map/ppermute | solution.py:217
  27.6 6.5 %collective-permute-start.2 = (bf16[224,512]{1,0:T(8,128)(2,1)S(1)}, bf16[224,512]{1,0:T(8,128)(2,1)S(1)}, u32[]{:S(2)}, u32[]{:S(2)}) collective-permute-start(bf16[224,512]{1,0:T(8,128)(2,1)S(1)} %get-tuple-element.27), channel_id=1, source_target_pairs={{0,24},{1,7},{2,26},{3,1},{4,28},{5,3},{6,30},{7,5},{8,0},{9,15},{... | collective-permute-start | bytes 688136 | tf_op jit(solution)/shard_map/ppermute | solution.py:217
  34.2 13.6 %collective-permute-start.3 = (bf16[4,224,512]{2,1,0:T(8,128)(2,1)S(1)}, bf16[4,224,512]{2,1,0:T(8,128)(2,1)}, u32[]{:S(2)}, u32[]{:S(2)}) collective-permute-start(bf16[4,224,512]{2,1,0:T(8,128)(2,1)S(1)} %pad_maximum_fusion.refs_0_), channel_id=1, source_target_pairs={{0,2},{1,9},{2,4},{3,11},{4,6},{5,13},{6,0},{7,15},{8,10},{9,17},{... | collective-permute-start | bytes 2752520 | tf_op jit(solution)/shard_map/ppermute | solution.py:219
  35.8 15.1 %collective-permute-start.4 = (bf16[4,224,512]{2,1,0:T(8,128)(2,1)S(1)}, bf16[4,224,512]{2,1,0:T(8,128)(2,1)}, u32[]{:S(2)}, u32[]{:S(2)}) collective-permute-start(bf16[4,224,512]{2,1,0:T(8,128)(2,1)S(1)} %pad_maximum_fusion.refs_0_), channel_id=1, source_target_pairs={{0,4},{1,17},{2,6},{3,19},{4,0},{5,21},{6,2},{7,23},{8,12},{9,25},... | collective-permute-start | bytes 2752520 | tf_op jit(solution)/shard_map/ppermute | solution.py:219
  36.7 23.3 %collective-permute-start.5 = (bf16[4,224,512]{2,1,0:T(8,128)(2,1)S(1)}, bf16[4,224,512]{2,1,0:T(8,128)(2,1)}, u32[]{:S(2)}, u32[]{:S(2)}) collective-permute-start(bf16[4,224,512]{2,1,0:T(8,128)(2,1)S(1)} %pad_maximum_fusion.refs_0_), channel_id=1, source_target_pairs={{0,6},{1,25},{2,0},{3,27},{4,2},{5,29},{6,4},{7,31},{8,14},{9,1},{... | collective-permute-start | bytes 2752520 | tf_op jit(solution)/shard_map/ppermute | solution.py:219
  39.2 28.7 %collective-permute-start.6 = (bf16[4,224,512]{2,1,0:T(8,128)(2,1)S(1)}, bf16[4,224,512]{2,1,0:T(8,128)(2,1)}, u32[]{:S(2)}, u32[]{:S(2)}) collective-permute-start(bf16[4,224,512]{2,1,0:T(8,128)(2,1)S(1)} %pad_maximum_fusion.refs_0_), channel_id=1, source_target_pairs={{0,1},{1,0},{2,3},{3,2},{4,5},{5,4},{6,7},{7,6},{8,9},{9,8},{10,11... | collective-permute-start | bytes 2752520 | tf_op jit(solution)/shard_map/ppermute | solution.py:34
  47.7 20.2 %collective-permute-start.7 = (bf16[4,224,512]{2,1,0:T(8,128)(2,1)}, bf16[4,224,512]{2,1,0:T(8,128)(2,1)}, u32[]{:S(2)}, u32[]{:S(2)}) collective-permute-start(bf16[4,224,512]{2,1,0:T(8,128)(2,1)} %collective-permute-done.3.refs_1_), channel_id=1, source_target_pairs={{0,1},{1,0},{2,3},{3,2},{4,5},{5,4},{6,7},{7,6},{8,9},{9,8},{10,11... | collective-permute-start | bytes 2752520 | tf_op jit(solution)/shard_map/ppermute | solution.py:34
  50.9 17.0 %collective-permute-start.8 = (bf16[4,224,512]{2,1,0:T(8,128)(2,1)}, bf16[4,224,512]{2,1,0:T(8,128)(2,1)}, u32[]{:S(2)}, u32[]{:S(2)}) collective-permute-start(bf16[4,224,512]{2,1,0:T(8,128)(2,1)} %collective-permute-done.4.refs_2_), channel_id=1, source_target_pairs={{0,1},{1,0},{2,3},{3,2},{4,5},{5,4},{6,7},{7,6},{8,9},{9,8},{10,11... | collective-permute-start | bytes 2752520 | tf_op jit(solution)/shard_map/ppermute | solution.py:34
  60.1 7.8 %collective-permute-start.9 = (bf16[4,224,512]{2,1,0:T(8,128)(2,1)}, bf16[4,224,512]{2,1,0:T(8,128)(2,1)}, u32[]{:S(2)}, u32[]{:S(2)}) collective-permute-start(bf16[4,224,512]{2,1,0:T(8,128)(2,1)} %collective-permute-done.5.refs_3_), channel_id=1, source_target_pairs={{0,1},{1,0},{2,3},{3,2},{4,5},{5,4},{6,7},{7,6},{8,9},{9,8},{10,11... | collective-permute-start | bytes 2752520 | tf_op jit(solution)/shard_map/ppermute | solution.py:34
  63.0 4.9 %copy-start.7 = (f32[7168]{0:T(1024)S(1)}, f32[7168]{0:T(1024)}, u32[]{:S(2)}) copy-start(f32[7168]{0:T(1024)} %param.11) | copy-start | bytes 86020
  63.0 9.1 %copy-start.3 = (bf16[152,7168]{1,0:T(8,128)(2,1)S(1)}, bf16[152,7168]{1,0:T(8,128)(2,1)}, u32[]{:S(2)}) copy-start(bf16[152,7168]{1,0:T(8,128)(2,1)} %refs_10_.1) | copy-start | bytes 6537220
  67.9 4.2 %copy-start.2 = (bf16[152,7168]{1,0:T(8,128)(2,1)S(1)}, bf16[152,7168]{1,0:T(8,128)(2,1)}, u32[]{:S(2)}) copy-start(bf16[152,7168]{1,0:T(8,128)(2,1)} %refs_9_.1) | copy-start | bytes 6537220
  72.1 1.6 %copy-start.4 = (bf16[1,152,7168]{2,1,0:T(8,128)(2,1)S(1)}, bf16[1,152,7168]{2,1,0:T(8,128)(2,1)}, u32[]{:S(2)}) copy-start(bf16[1,152,7168]{2,1,0:T(8,128)(2,1)} %param.17) | copy-start | bytes 6537220
  73.7 14.9 %copy-start = (bf16[152,7168]{0,1:T(8,128)(2,1)S(1)}, bf16[152,7168]{0,1:T(8,128)(2,1)}, u32[]{:S(2)}) copy-start(bf16[152,7168]{0,1:T(8,128)(2,1)} %copy.40) | copy-start | bytes 6537220
  73.7 14.9 %copy-start.1 = (bf16[1,152,7168]{1,2,0:T(8,128)(2,1)S(1)}, bf16[1,152,7168]{1,2,0:T(8,128)(2,1)}, u32[]{:S(2)}) copy-start(bf16[1,152,7168]{1,2,0:T(8,128)(2,1)} %copy.41) | copy-start | bytes 6537220
  90.6 7.2 %collective-permute-start.11 = (bf16[4,224,512]{2,1,0:T(8,128)(2,1)S(1)}, bf16[4,224,512]{2,1,0:T(8,128)(2,1)S(1)}, u32[]{:S(2)}, u32[]{:S(2)}) collective-permute-start(bf16[4,224,512]{2,1,0:T(8,128)(2,1)S(1)} %get-tuple-element.16), channel_id=1, source_target_pairs={{0,1},{1,0},{2,3},{3,2},{4,5},{5,4},{6,7},{7,6},{8,9},{9,8},{10,11... | collective-permute-start | bytes 2752520 | tf_op jit(solution)/shard_map/ppermute | solution.py:34
  93.2 6.1 %collective-permute-start.13 = (bf16[4,224,512]{2,1,0:T(8,128)(2,1)S(1)}, bf16[4,224,512]{2,1,0:T(8,128)(2,1)S(1)}, u32[]{:S(2)}, u32[]{:S(2)}) collective-permute-start(bf16[4,224,512]{2,1,0:T(8,128)(2,1)S(1)} %get-tuple-element.18), channel_id=1, source_target_pairs={{0,1},{1,0},{2,3},{3,2},{4,5},{5,4},{6,7},{7,6},{8,9},{9,8},{10,11... | collective-permute-start | bytes 2752520 | tf_op jit(solution)/shard_map/ppermute | solution.py:34
  95.2 6.3 %collective-permute-start.15 = (bf16[4,224,512]{2,1,0:T(8,128)(2,1)S(1)}, bf16[4,224,512]{2,1,0:T(8,128)(2,1)S(1)}, u32[]{:S(2)}, u32[]{:S(2)}) collective-permute-start(bf16[4,224,512]{2,1,0:T(8,128)(2,1)S(1)} %get-tuple-element.20), channel_id=1, source_target_pairs={{0,1},{1,0},{2,3},{3,2},{4,5},{5,4},{6,7},{7,6},{8,9},{9,8},{10,11... | collective-permute-start | bytes 2752520 | tf_op jit(solution)/shard_map/ppermute | solution.py:34
  97.7 5.4 %collective-permute-start.10 = (bf16[4,224,512]{2,1,0:T(8,128)(2,1)S(1)}, bf16[4,224,512]{2,1,0:T(8,128)(2,1)S(1)}, u32[]{:S(2)}, u32[]{:S(2)}) collective-permute-start(bf16[4,224,512]{2,1,0:T(8,128)(2,1)S(1)} %get-tuple-element.14), channel_id=1, source_target_pairs={{0,1},{1,0},{2,3},{3,2},{4,5},{5,4},{6,7},{7,6},{8,9},{9,8},{10,11... | collective-permute-start | bytes 2752520 | tf_op jit(solution)/shard_map/ppermute | solution.py:34
  98.1 13.5 %collective-permute-start.12 = (bf16[4,224,512]{2,1,0:T(8,128)(2,1)S(1)}, bf16[4,224,512]{2,1,0:T(8,128)(2,1)S(1)}, u32[]{:S(2)}, u32[]{:S(2)}) collective-permute-start(bf16[4,224,512]{2,1,0:T(8,128)(2,1)S(1)} %add_convert_fusion.2), channel_id=1, source_target_pairs={{0,2},{1,9},{2,4},{3,11},{4,6},{5,13},{6,0},{7,15},{8,10},{9,17},{... | collective-permute-start | bytes 2752520 | tf_op jit(solution)/shard_map/ppermute | solution.py:234
  99.6 15.1 %collective-permute-start.14 = (bf16[4,224,512]{2,1,0:T(8,128)(2,1)S(1)}, bf16[4,224,512]{2,1,0:T(8,128)(2,1)S(1)}, u32[]{:S(2)}, u32[]{:S(2)}) collective-permute-start(bf16[4,224,512]{2,1,0:T(8,128)(2,1)S(1)} %add_convert_fusion.1), channel_id=1, source_target_pairs={{0,4},{1,17},{2,6},{3,19},{4,0},{5,21},{6,2},{7,23},{8,12},{9,25},... | collective-permute-start | bytes 2752520 | tf_op jit(solution)/shard_map/ppermute | solution.py:234
  101.8 22.7 %collective-permute-start.16 = (bf16[4,224,512]{2,1,0:T(8,128)(2,1)S(1)}, bf16[4,224,512]{2,1,0:T(8,128)(2,1)S(1)}, u32[]{:S(2)}, u32[]{:S(2)}) collective-permute-start(bf16[4,224,512]{2,1,0:T(8,128)(2,1)S(1)} %add_convert_fusion), channel_id=1, source_target_pairs={{0,6},{1,25},{2,0},{3,27},{4,2},{5,29},{6,4},{7,31},{8,14},{9,1},{... | collective-permute-start | bytes 2752520 | tf_op jit(solution)/shard_map/ppermute | solution.py:234
  125.2 7.3 %collective-permute-start.17 = (bf16[224,512]{1,0:T(8,128)(2,1)S(1)}, bf16[224,512]{1,0:T(8,128)(2,1)S(1)}, u32[]{:S(2)}, u32[]{:S(2)}) collective-permute-start(bf16[224,512]{1,0:T(8,128)(2,1)S(1)} %get-tuple-element.23), channel_id=1, source_target_pairs={{0,8},{1,3},{2,10},{3,5},{4,12},{5,7},{6,14},{7,1},{8,16},{9,11},{... | collective-permute-start | bytes 688136 | tf_op jit(solution)/shard_map/ppermute | solution.py:237
  127.2 8.6 %collective-permute-start.18 = (bf16[224,512]{1,0:T(8,128)(2,1)S(1)}, bf16[224,512]{1,0:T(8,128)(2,1)S(1)}, u32[]{:S(2)}, u32[]{:S(2)}) collective-permute-start(bf16[224,512]{1,0:T(8,128)(2,1)S(1)} %get-tuple-element.25), channel_id=1, source_target_pairs={{0,16},{1,5},{2,18},{3,7},{4,20},{5,1},{6,22},{7,3},{8,24},{9,13},... | collective-permute-start | bytes 688136 | tf_op jit(solution)/shard_map/ppermute | solution.py:237
  129.3 6.5 %collective-permute-start.19 = (bf16[224,512]{1,0:T(8,128)(2,1)S(1)}, bf16[224,512]{1,0:T(8,128)(2,1)S(1)}, u32[]{:S(2)}, u32[]{:S(2)}) collective-permute-start(bf16[224,512]{1,0:T(8,128)(2,1)S(1)} %get-tuple-element.24), channel_id=1, source_target_pairs={{0,24},{1,7},{2,26},{3,1},{4,28},{5,3},{6,30},{7,5},{8,0},{9,15},{... | collective-permute-start | bytes 688136 | tf_op jit(solution)/shard_map/ppermute | solution.py:237
  135.8 4.6 %copy-start.8 = (f32[128,2]{0,1:T(2,128)S(1)}, f32[128,2]{0,1:T(2,128)}, u32[]{:S(2)}) copy-start(f32[128,2]{0,1:T(2,128)} %param.13) | copy-start | bytes 3076
  136.9 16.3 %all-to-all-start.1 = ((f32[8,48,224]{2,1,0:T(8,128)}), f32[8,48,224]{2,1,0:T(8,128)S(1)}, u32[]{:S(2)}, u32[]{:S(2)}) async-start(f32[8,48,224]{2,1,0:T(8,128)} %bitcast.25), calls=%async_computation.1 | async-start | bytes 786432 | tf_op jit(solution)/shard_map/all_to_all | solution.py:240

commit v2 on v0

v2 whole, which is shorter than its diff:
```python
import functools

import jax
import jax.numpy as jnp
from jax import lax
from jax.experimental import pallas as pl
from jax.experimental.pallas import tpu as pltpu
from jax.sharding import PartitionSpec as P

SIDE = 4
PAIR = 2
CHIPS = SIDE * SIDE
GROUP = CHIPS * PAIR
F32 = jnp.float32
BF16 = jnp.bfloat16
MIB = 1024 * 1024


def device_of(x, y, core):
    return (x * SIDE + y) * PAIR + core


def hops(step, first):
    pairs = []
    for x in range(SIDE):
        for y in range(SIDE):
            for core in range(PAIR):
                along_x = (core == 0) == first
                to_x = (x + step) % SIDE if along_x else x
                to_y = y if along_x else (y + step) % SIDE
                pairs.append((device_of(x, y, core), device_of(to_x, to_y, core)))
    return pairs


def sibling(value):
    return lax.ppermute(value, "tensor", [(i, i ^ 1) for i in range(GROUP)])


def piece_index(place, other, sign, outer, inner):
    x, y, core = place[0], place[1], place[2]
    owner = 1 - core if other else core
    move_x = jnp.where(owner == 0, inner, outer)
    move_y = jnp.where(owner == 0, outer, inner)
    at_x = lax.rem(x + sign * move_x + SIDE, SIDE)
    at_y = lax.rem(y + sign * move_y + SIDE, SIDE)
    return device_of(at_x, at_y, owner)


def dispatch_kernel(experts, capacity, ids, probs, tokens, outgoing, combine):
    choose, rows = ids.shape
    slots = experts * capacity
    numbers = lax.broadcasted_iota(jnp.int32, (experts, rows), 0)
    before = lax.broadcasted_iota(jnp.int32, (rows, rows), 0)
    after = lax.broadcasted_iota(jnp.int32, (rows, rows), 1)
    earlier = (before < after).astype(F32).astype(BF16)
    slot_numbers = lax.broadcasted_iota(jnp.int32, (slots, rows), 0)
    taken = jnp.zeros((experts, 1), F32)
    weights = jnp.zeros((slots, rows), F32)
    chosen = jnp.zeros((slots, rows), F32)
    for k in range(choose):
        named = ids[k : k + 1, :]
        onehot = (numbers == named).astype(F32)
        ahead = jnp.dot(onehot.astype(BF16), earlier, preferred_element_type=F32) + taken
        position = jnp.sum(ahead * onehot, axis=0, keepdims=True).astype(jnp.int32)
        hits = slot_numbers == named * capacity + position
        weights = weights + jnp.where(hits, probs[k : k + 1, :], 0.0)
        chosen = chosen + hits.astype(F32)
        taken = taken + jnp.sum(onehot, axis=1, keepdims=True)
    combine[...] = weights
    outgoing[...] = lax.dot_general(
        chosen.astype(BF16), tokens[...], (((1,), (1,)), ((), ())), preferred_element_type=F32
    ).astype(BF16)


def dispatched(ids, probs, tokens, experts, capacity):
    cols, rows = tokens.shape
    return pl.pallas_call(
        functools.partial(dispatch_kernel, experts, capacity),
        out_shape=(
            jax.ShapeDtypeStruct((experts * capacity, cols), BF16),
            jax.ShapeDtypeStruct((experts * capacity, rows), F32),
        ),
        name="dispatch",
    )(ids, probs, tokens)


def weights_kernel(cols, gain, *refs):
    ins, outs = refs[:6], refs[6:]
    for i in range(ins[0].shape[1] // cols):
        at = slice(i * cols, (i + 1) * cols)
        for gate, up, out in ((ins[0], ins[1], outs[0]), (ins[2], ins[3], outs[1])):
            both = jnp.concatenate([gate[:, at].astype(F32), up[:, at].astype(F32)], axis=0)
            out[i] = (both * gain[:, at]).astype(BF16)
        for down, out in ((ins[4], outs[2]), (ins[5], outs[3])):
            out[i] = down[:, at].astype(F32).T.astype(BF16)


def piece_weights(gain, dense_gate, dense_up, expert_gate, expert_up, dense_down, expert_down, cols):
    units, width = dense_gate.shape
    each = 4
    wide = pl.BlockSpec((units, each * cols), lambda i: (0, i))
    up_shape = jax.ShapeDtypeStruct((width // cols, 2 * units, cols), BF16)
    down_shape = jax.ShapeDtypeStruct((width // cols, cols, units), BF16)
    return pl.pallas_call(
        functools.partial(weights_kernel, cols),
        out_shape=(up_shape, up_shape, down_shape, down_shape),
        grid=(width // (each * cols),),
        in_specs=[pl.BlockSpec((1, each * cols), lambda i: (0, i))] + [wide] * 6,
        out_specs=[pl.BlockSpec((each, 2 * units, cols), lambda i: (i, 0, 0))] * 2
        + [pl.BlockSpec((each, cols, units), lambda i: (i, 0, 0))] * 2,
        compiler_params=pltpu.CompilerParams(vmem_limit_bytes=56 * MIB),
        cost_estimate=pl.CostEstimate(flops=12 * units * width, bytes_accessed=28 * MIB, transcendentals=0),
        name="piece_weights",
    )(gain, dense_gate, dense_up, expert_gate, expert_up, dense_down, expert_down)


def arrive_kernel(dense_rows, count, start, last, width, place, *refs):
    stacks, refs = refs[:count], refs[count:]
    dense, routed, refs = refs[:count], refs[count : 2 * count], refs[2 * count :]
    if not start:
        carried, refs = refs[:3], refs[3:]
    if last:
        hidden, refs = refs[0], refs[1:]
    dense_sum, routed_sum, squares = refs

    @pl.when(pl.program_id(0) == 0)
    def _():
        for i, ref in enumerate((dense_sum, routed_sum, squares)):
            ref[...] = jnp.zeros_like(ref) if start else carried[i][...]

    for j in range(count):
        block = stacks[j][0]
        dense_sum[...] += jnp.dot(dense[j][0], block[:, :dense_rows], preferred_element_type=F32)
        routed_sum[...] += jnp.dot(routed[j][0], block[:, dense_rows:], preferred_element_type=F32)
        values = block.astype(F32)
        values = values * values
        squares[...] += jnp.sum(values.reshape(values.shape[0] // 8, 8, values.shape[1]), axis=0)

    if last:

        @pl.when(pl.program_id(0) == pl.num_programs(0) - 1)
        def _():
            scale = lax.rsqrt(jnp.sum(squares[...], axis=0, keepdims=True) / width + 1e-05)
            units = dense_sum.shape[0] // 2
            for sums, span in (
                (dense_sum, slice(0, dense_rows)),
                (routed_sum, slice(dense_rows, scale.shape[1])),
            ):
                gates = sums[:units, :] * scale[:, span]
                ups = sums[units:, :] * scale[:, span]
                hidden[:, span] = (gates / (1.0 + jnp.exp(-gates)) * ups).astype(BF16)


def arrive(place, stage, dense, routed, sums, dense_rows, last=False):
    count = len(stage)
    cols, rows = stage[0][0].shape[1:]
    height = dense.shape[1]
    start = sums is None

    def weight(outer, other):
        def index(i, place):
            return piece_index(place, other, -1, outer, i), 0, 0

        return pl.BlockSpec((1, height, cols), index)

    whole = lambda shape: pl.BlockSpec(shape, lambda i, place: (0, 0))
    shapes = [(height, dense_rows), (height, rows - dense_rows), (8, rows)]
    sum_specs = [whole(s) for s in shapes]
    sum_shapes = [jax.ShapeDtypeStruct(s, F32) for s in shapes]
    hidden_shape = (height // 2, rows)
    if last:
        out_specs, out_shape, scratch = (
            whole(hidden_shape),
            jax.ShapeDtypeStruct(hidden_shape, BF16),
            [pltpu.VMEM(s, F32) for s in shapes],
        )
    else:
        out_specs, out_shape, scratch = sum_specs, sum_shapes, []
    weights = [weight(outer, other) for _, outer, other in stage]
    return pl.pallas_call(
        functools.partial(arrive_kernel, dense_rows, count, start, last, GROUP * cols),
        out_shape=out_shape,
        grid_spec=pltpu.PrefetchScalarGridSpec(
            num_scalar_prefetch=1,
            grid=(SIDE,),
            in_specs=[pl.BlockSpec((1, cols, rows), lambda i, place: (i, 0, 0))] * count
            + weights * 2
            + ([] if start else sum_specs),
            out_specs=out_specs,
            scratch_shapes=scratch,
        ),
        compiler_params=pltpu.CompilerParams(vmem_limit_bytes=24 * MIB),
        cost_estimate=pl.CostEstimate(
            flops=2 * SIDE * count * height * cols * rows,
            bytes_accessed=2 * MIB * count,
            transcendentals=0,
        ),
        name=f"arrive_{stage[-1][1]}_{count}",
    )(
        place,
        *[stack for stack, _, _ in stage],
        *[dense] * count,
        *[routed] * count,
        *([] if start else sums),
    )


def down_kernel(dense_rows, place, hidden, *refs):
    for half in range(2):
        dense, routed, out = refs[2 * half], refs[2 * half + 1], refs[4 + half]
        for weight, span in (
            (dense, slice(0, dense_rows)),
            (routed, slice(dense_rows, hidden.shape[1])),
        ):
            out[0, :, span] = jnp.dot(
                weight[0], hidden[:, span], preferred_element_type=F32
            ).astype(out.dtype)


def down_pieces(place, hidden, dense_down, expert_down, outer, dense_rows):
    units, rows = hidden.shape
    cols = dense_down.shape[1]

    def weight(other):
        def index(i, place):
            return piece_index(place, other, 1, outer, i), 0, 0

        return pl.BlockSpec((1, cols, units), index)

    out = pl.BlockSpec((1, cols, rows), lambda i, place: (i, 0, 0))
    shape = (SIDE, cols, rows)
    return pl.pallas_call(
        functools.partial(down_kernel, dense_rows),
        out_shape=(jax.ShapeDtypeStruct(shape, F32), jax.ShapeDtypeStruct(shape, BF16)),
        grid_spec=pltpu.PrefetchScalarGridSpec(
            num_scalar_prefetch=1,
            grid=(SIDE,),
            in_specs=[pl.BlockSpec((units, rows), lambda i, place: (0, 0))]
            + [weight(False)] * 2
            + [weight(True)] * 2,
            out_specs=(out, out),
        ),
        compiler_params=pltpu.CompilerParams(vmem_limit_bytes=16 * MIB),
        cost_estimate=pl.CostEstimate(
            flops=4 * SIDE * cols * rows * units, bytes_accessed=4 * MIB, transcendentals=0
        ),
        name=f"down_pieces_{outer}",
    )(place, hidden, dense_down, expert_down, dense_down, expert_down)


def shards(
    tokens,
    norm_gain,
    route_ids,
    route_probs,
    dense_gate,
    dense_up,
    dense_down,
    expert_gate,
    expert_up,
    expert_down,
):
    experts = lax.axis_size("expert")
    rows, choose = route_ids.shape
    cols = tokens.shape[1]
    capacity = 3 * rows * choose // (2 * experts)
    index = lax.axis_index("tensor")
    place = jnp.stack([index // (SIDE * PAIR), index // PAIR % SIDE, index % PAIR]).astype(jnp.int32)

    outgoing, combine = dispatched(route_ids.T, route_probs.T, tokens.T, experts, capacity)
    received = lax.all_to_all(
        outgoing.reshape(experts, capacity, cols), "expert", 0, 0, tiled=True
    ).reshape(experts * capacity, cols)
    own = jnp.concatenate([tokens.T, received.T], axis=1)

    first = [own] + [lax.ppermute(own, "tensor", hops(d, True)) for d in range(1, SIDE)]
    stack = jnp.stack(first)
    near, far, left = [lax.ppermute(stack, "tensor", hops(d, False)) for d in (1, 2, 3)]
    stack_other = sibling(stack)
    dense, routed, dense_down, routed_down = piece_weights(
        norm_gain[None, :],
        dense_gate,
        dense_up,
        expert_gate[0],
        expert_up[0],
        dense_down,
        expert_down[0],
        cols,
    )
    add = functools.partial(arrive, place, dense=dense, routed=routed, dense_rows=rows)
    sums = add([(stack, 0, False)], sums=None)
    near, stack_other, sums, dense_down, routed_down = lax.optimization_barrier(
        (near, stack_other, sums, dense_down, routed_down)
    )
    near_other = sibling(near)
    sums = add([(stack_other, 0, True), (near, 1, False)], sums=sums)
    far, left, sums = lax.optimization_barrier((far, left, sums))
    far_other, left_other = sibling(far), sibling(left)
    sums = add([(near_other, 1, True), (far, 2, False), (left, 3, False)], sums=sums)
    far_other, left_other, sums = lax.optimization_barrier((far_other, left_other, sums))
    hidden = add([(far_other, 2, True), (left_other, 3, True)], sums=sums, last=True)

    pieces = {}
    for outer in (1, 2, 3, 0):
        mine, others = down_pieces(place, hidden, dense_down, routed_down, outer, rows)
        if outer > 1:
            pieces[outer - 1], hidden = lax.optimization_barrier((pieces[outer - 1], hidden))
        pieces[outer] = mine + sibling(others).astype(F32)
    level = pieces[0]
    level = pieces[0]
    for d in range(1, SIDE):
        level = level + lax.ppermute(pieces[d].astype(BF16), "tensor", hops(d, False)).astype(F32)
    total = level[0]
    for d in range(1, SIDE):
        total = total + lax.ppermute(level[d].astype(BF16), "tensor", hops(d, True)).astype(F32)

    back = total[:, rows:].astype(BF16).T.reshape(experts, capacity, cols)
    returned = lax.all_to_all(back, "expert", 0, 0, tiled=True).reshape(experts * capacity, cols)
    moe_out = jnp.dot(combine.T, returned.astype(F32), precision=lax.Precision.HIGHEST)
    return (total[:, :rows].T + moe_out).astype(BF16)


def solution(mesh):
    in_specs = (
        P("expert", "tensor"),
        P(),
        P("expert", None),
        P("expert", None),
        P("tensor", None),
        P("tensor", None),
        P("tensor", None),
        P("expert", "tensor", None),
        P("expert", "tensor", None),
        P("expert", "tensor", None),
    )
    out_specs = P("expert", "tensor")
    return jax.shard_map(shards, mesh=mesh, in_specs=in_specs, out_specs=out_specs, check_vma=False)
```

time: 365 us -> 133 us (0.36)
  waiting for transfers between devices: 292 us -> 32.4 us
  Pallas kernels: 0 us -> 36.3 us
  blocking collectives: 0 us -> 31.1 us
  matrix products: 25.4 us -> 0.99 us
  between operations: 13.3 us -> 0.21 us
  other arithmetic: 7.31 us -> 2.82 us
    reduce_scatter x2 -> x0, waiting for transfers between devices: 159 us -> none  [the longest x1 95.9 us: shards(): lax.psum_scatter(partial_value, 'tensor', scatter_dimension=1, tiled=True)]
    all_gather x2 -> x0, waiting for transfers between devices: 104 us -> none  [the longest x1 52.9 us: shards(): piece = lax.all_gather(received, 'tensor', axis=1, tiled=True)]
    pallas_call x0 -> x10, Pallas kernels: none -> 36.3 us  [the longest x1 15.7 us: piece_weights(): pl.pallas_call(functools.partial(weights_kernel, cols), out_shape=(up_sha...]
    all_to_all x0 -> x2, blocking collectives: none -> 31.1 us  [the longest x1 18.9 us: shards(): lax.all_to_all(outgoing.reshape(experts, capacity, cols), 'expert', 0, 0,...]
    dot_general x7 -> x1, matrix products: 25.4 us -> 0.99 us  [shards(): jnp.dot(combine.T, returned.astype(F32), precision=lax.Precision.HIGHEST)]
    ppermute x6 -> x20, waiting for transfers between devices: 28.6 us -> 32.4 us  [the longest x3 21 us: shards(): lax.ppermute(pieces[d].astype(BF16), 'tensor', hops(d, False)).astype(F32)]
    ppermute x6 -> x20, starting transfers between devices: 20.2 us -> 22.2 us  [the longest x3 5.73 us: shards(): lax.ppermute(own, 'tensor', hops(d, True))]
  transfers between devices with their start and end apart: 10 -> 20, of which waited for: 10 -> 8; matrix products, arithmetic and copies ran while one was open for 4% -> 1% of each run, Pallas kernels for 0% -> 23%
where the time goes in v2:
time: 133 us; the launch traced here: 132 us
  Pallas kernels  36.3 us (27%)
  waiting for transfers between devices  32.4 us (24%)
  blocking collectives  31.1 us (23%)
  starting transfers between devices  22.2 us (17%)
  local copies, waits for them, and re-layouts  5.86 us (4%)
  other arithmetic  2.82 us (2%)
    ppermute x3, waiting for transfers between devices, shards(): lax.ppermute(pieces[d].astype(BF16), 'tensor', hops(d, False)).astype(F32)  21 us
    all_to_all x1, blocking collectives, shards(): lax.all_to_all(outgoing.reshape(experts, capacity, cols), 'expert', 0, 0,...  18.9 us
    pallas_call x1, Pallas kernels, piece_weights(): pl.pallas_call(functools.partial(weights_kernel, cols), out_shape=(up_sha...  15.7 us
    all_to_all x1, blocking collectives, shards(): lax.all_to_all(back, 'expert', 0, 0, tiled=True)  12.2 us
    pallas_call x4, Pallas kernels, arrive(): pl.pallas_call(functools.partial(arrive_kernel, dense_rows, count, start,...  11.2 us
    pallas_call x4, Pallas kernels, down_pieces(): pl.pallas_call(functools.partial(down_kernel, dense_rows), out_shape=(jax...  7.52 us
    ppermute x3, waiting for transfers between devices, shards(): lax.ppermute(level[d].astype(BF16), 'tensor', hops(d, True)).astype(F32)  5.99 us
    ppermute x3, starting transfers between devices, shards(): lax.ppermute(own, 'tensor', hops(d, True))  5.73 us
  transfers between devices with their start and end apart: 20, of which 8 were waited for; matrix products, arithmetic and copies ran while one was open for 1% of the time, Pallas kernels for 23%

profile of v2, /device:TPU:8, one launch (start us, length us, event | category | flops | bytes accessed | tf_op | source)
XLA Modules:
  0.0 131.8 jit_solution(16109174053565330021)
XLA Ops:
  0.0 1.9 %dispatch.1 = (bf16[384,224]{1,0:T(8,128)(2,1)}, f32[384,128]{1,0:T(8,128)}) custom-call(s32[2,128]{1,0:T(2,128)} %bitcast.58, f32[2,128]{1,0:T(2,128)} %bitcast.59, bf16[224,128]{1,0:T(8,128)(2,1)} %bitcast.54), custom_call_target="tpu_custom_call" | custom-call | tf_op jit(solution)/shard_map/dispatch/pallas_call | solution.py:77
  1.9 18.9 %all_to_all.10 = bf16[8,48,224]{2,1,0:T(8,128)(2,1)S(1)} all-to-all(bf16[8,48,224]{2,1,0:T(8,128)(2,1)} %bitcast.56), channel_id=1, replica_groups=mesh['expert'=8,'tensor'=32] {'expert'}, dimensions={0} | all-to-all | bytes 344064 | tf_op jit(solution)/shard_map/all_to_all | solution.py:271
  20.8 0.1 copy.12
  20.9 0.9 fusion.6
  21.8 1.6 %collective-permute-start = (bf16[224,512]{1,0:T(8,128)(2,1)S(1)}, bf16[224,512]{1,0:T(8,128)(2,1)S(1)}, u32[]{:S(2)}, u32[]{:S(2)}) collective-permute-start(bf16[224,512]{1,0:T(8,128)(2,1)S(1)} %get-tuple-element.99), channel_id=1, source_target_pairs={{0,8},{1,3},{2,10},{3,5},{4,12},{5,7},{6,14},{7,1},{8,16},{9,11},{... | collective-permute-start | bytes 688136 | tf_op jit(solution)/shard_map/ppermute | solution.py:276
  23.4 2.7 %collective-permute-start.1 = (bf16[224,512]{1,0:T(8,128)(2,1)S(1)}, bf16[224,512]{1,0:T(8,128)(2,1)S(1)}, u32[]{:S(2)}, u32[]{:S(2)}) collective-permute-start(bf16[224,512]{1,0:T(8,128)(2,1)S(1)} %get-tuple-element.99), channel_id=1, source_target_pairs={{0,16},{1,5},{2,18},{3,7},{4,20},{5,1},{6,22},{7,3},{8,24},{9,13},... | collective-permute-start | bytes 688136 | tf_op jit(solution)/shard_map/ppermute | solution.py:276
  26.1 1.4 %collective-permute-start.2 = (bf16[224,512]{1,0:T(8,128)(2,1)S(1)}, bf16[224,512]{1,0:T(8,128)(2,1)S(1)}, u32[]{:S(2)}, u32[]{:S(2)}) collective-permute-start(bf16[224,512]{1,0:T(8,128)(2,1)S(1)} %get-tuple-element.99), channel_id=1, source_target_pairs={{0,24},{1,7},{2,26},{3,1},{4,28},{5,3},{6,30},{7,5},{8,0},{9,15},{... | collective-permute-start | bytes 688136 | tf_op jit(solution)/shard_map/ppermute | solution.py:276
  27.5 1.6 %collective-permute-done = bf16[224,512]{1,0:T(8,128)(2,1)S(1)} collective-permute-done((bf16[224,512]{1,0:T(8,128)(2,1)S(1)}, bf16[224,512]{1,0:T(8,128)(2,1)S(1)}, u32[]{:S(2)}, u32[]{:S(2)}) %collective-permute-start) | collective-permute-done | bytes 229408 | tf_op jit(solution)/shard_map/ppermute | solution.py:276
  29.1 3.4 %collective-permute-done.1 = bf16[224,512]{1,0:T(8,128)(2,1)S(1)} collective-permute-done((bf16[224,512]{1,0:T(8,128)(2,1)S(1)}, bf16[224,512]{1,0:T(8,128)(2,1)S(1)}, u32[]{:S(2)}, u32[]{:S(2)}) %collective-permute-start.1) | collective-permute-done | bytes 229408 | tf_op jit(solution)/shard_map/ppermute | solution.py:276
  32.6 0.0 collective-permute-done.2
  32.6 0.1 pad_maximum_fusion.refs_0_
  32.7 1.7 %collective-permute-start.5 = (bf16[4,224,512]{2,1,0:T(8,128)(2,1)S(1)}, bf16[4,224,512]{2,1,0:T(8,128)(2,1)}, u32[]{:S(2)}, u32[]{:S(2)}) collective-permute-start(bf16[4,224,512]{2,1,0:T(8,128)(2,1)S(1)} %pad_maximum_fusion.refs_0_), channel_id=1, source_target_pairs={{0,2},{1,9},{2,4},{3,11},{4,6},{5,13},{6,0},{7,15},{8,10},{9,17},{... | collective-permute-start | bytes 2752520 | tf_op jit(solution)/shard_map/ppermute | solution.py:278
  34.3 0.0 collective-permute-start.6
  34.3 0.9 collective-permute-start.3
  35.3 2.4 %collective-permute-start.4 = (bf16[4,224,512]{2,1,0:T(8,128)(2,1)S(1)}, bf16[4,224,512]{2,1,0:T(8,128)(2,1)S(1)}, u32[]{:S(2)}, u32[]{:S(2)}) collective-permute-start(bf16[4,224,512]{2,1,0:T(8,128)(2,1)S(1)} %pad_maximum_fusion.refs_0_), channel_id=1, source_target_pairs={{0,6},{1,25},{2,0},{3,27},{4,2},{5,29},{6,4},{7,31},{8,14},{9,1},{... | collective-permute-start | bytes 2752520 | tf_op jit(solution)/shard_map/ppermute | solution.py:278
  37.7 15.7 %piece_weights.1 = (bf16[32,304,224]{2,1,0:T(8,128)(2,1)}, bf16[32,304,224]{2,1,0:T(8,128)(2,1)}, bf16[32,224,152]{2,1,0:T(8,128)(2,1)}, bf16[32,224,152]{2,1,0:T(8,128)(2,1)}) custom-call(f32[1,7168]{1,0:T(1,128)} %bitcast.57, bf16[152,7168]{1,0:T(8,128)(2,1)} %refs_0_.1, bf16[152,7168]{1,0:T(8,128)(2,1)} %refs_1_.1, bf16[152,7168]{1,0:T(8,128)(2,1)} %bitcast.44, ...), custom_call_target="tpu_custom_call" | custom-call | flops 13074432 | bytes 29360128 | tf_op jit(solution)/shard_map/piece_weights/pallas_call | solution.py:104
  53.4 0.1 pad_add_fusion.place
  53.5 2.4 %copy-done = bf16[32,304,224]{2,1,0:T(8,128)(2,1)S(1)} copy-done((bf16[32,304,224]{2,1,0:T(8,128)(2,1)S(1)}, bf16[32,304,224]{2,1,0:T(8,128)(2,1)}, u32[]{:S(2)}) %copy-start) | copy-done | bytes 4358168
  55.9 2.4 %copy-done.1 = bf16[32,304,224]{2,1,0:T(8,128)(2,1)S(1)} copy-done((bf16[32,304,224]{2,1,0:T(8,128)(2,1)S(1)}, bf16[32,304,224]{2,1,0:T(8,128)(2,1)}, u32[]{:S(2)}) %copy-start.1) | copy-done | bytes 4358168
  58.3 1.8 %arrive_0_1.1 = (f32[304,128]{1,0:T(8,128)S(1)}, f32[304,384]{1,0:T(8,128)S(1)}, f32[8,512]{1,0:T(8,128)S(1)}) custom-call(s32[3]{0:T(128)S(1)} %pad_add_fusion.place, bf16[4,224,512]{2,1,0:T(8,128)(2,1)S(1)} %pad_maximum_fusion.refs_0_, bf16[32,304,224]{2,1,0:T(8,128)(2,1)S(1)} %copy-done, bf16[32,304,224]{2,1,0:T(8,128)(2,1)S(1)} %copy-done.1), custom_call_target="tpu_custom_call" | custom-call | flops 278921216 | bytes 2097152 | tf_op jit(solution)/shard_map/arrive_0_1/pallas_call | solution.py:180
  60.1 0.0 collective-permute-done.5.refs_1_
  60.1 0.0 collective-permute-done.6.refs_0_
  60.1 1.2 collective-permute-start.9
  61.3 4.0 %arrive_1_2.1 = (f32[304,128]{1,0:T(8,128)S(1)}, f32[304,384]{1,0:T(8,128)S(1)}, f32[8,512]{1,0:T(8,128)S(1)}) custom-call(s32[3]{0:T(128)S(1)} %pad_add_fusion.place, bf16[4,224,512]{2,1,0:T(8,128)(2,1)} %collective-permute-done.6.refs_0_, bf16[4,224,512]{2,1,0:T(8,128)(2,1)} %collective-permute-done.5.refs_1_, bf16[32,304,224]{2,1,0:T(8,128)(2,1)S(1)} %copy-done, ...), custom_call_target="tpu_custom_call" | custom-call | flops 557842432 | bytes 4194304 | tf_op jit(solution)/shard_map/arrive_1_2/pallas_call | solution.py:180
  65.4 0.0 collective-permute-done.3.refs_1_
  65.4 0.0 collective-permute-done.4.refs_2_
  65.4 0.1 collective-permute-start.7
  65.5 0.5 collective-permute-start.8
  66.0 0.0 collective-permute-done.9.refs_0_
  66.0 2.9 %arrive_3_3.1 = (f32[304,128]{1,0:T(8,128)S(1)}, f32[304,384]{1,0:T(8,128)S(1)}, f32[8,512]{1,0:T(8,128)S(1)}) custom-call(s32[3]{0:T(128)S(1)} %pad_add_fusion.place, bf16[4,224,512]{2,1,0:T(8,128)(2,1)S(1)} %collective-permute-done.9.refs_0_, bf16[4,224,512]{2,1,0:T(8,128)(2,1)S(1)} %collective-permute-done.3.refs_1_, ...), custom_call_target="tpu_custom_call" | custom-call | flops 836763648 | bytes 6291456 | tf_op jit(solution)/shard_map/arrive_3_3/pallas_call | solution.py:180
  68.9 0.0 collective-permute-done.7.refs_0_
  68.9 0.4 collective-permute-done.8.refs_1_
  69.3 2.5 %arrive_3_2.1.hidden = bf16[152,512]{1,0:T(8,128)(2,1)S(1)} custom-call(s32[3]{0:T(128)S(1)} %pad_add_fusion.place, bf16[4,224,512]{2,1,0:T(8,128)(2,1)S(1)} %collective-permute-done.7.refs_0_, bf16[4,224,512]{2,1,0:T(8,128)(2,1)S(1)} %collective-permute-done.8.refs_1_, bf16[32,304,224]{2,1,0:T(8,128)(2,1)S(1)} %copy-done, ...), custom_call_target="tpu_custom_call" | custom-call | flops 557842432 | bytes 4194304 | tf_op jit(solution)/shard_map/arrive_3_2/pallas_call | solution.py:180
  71.8 0.7 copy-done.3
  72.4 1.9 %down_pieces_1.1 = (f32[4,224,512]{2,1,0:T(8,128)S(1)}, bf16[4,224,512]{2,1,0:T(8,128)(2,1)S(1)}) custom-call(s32[3]{0:T(128)S(1)} %pad_add_fusion.place, bf16[152,512]{1,0:T(8,128)(2,1)S(1)} %arrive_3_2.1.hidden, bf16[32,224,152]{2,1,0:T(8,128)(2,1)S(1)} %copy-done.2, bf16[32,224,152]{2,1,0:T(8,128)(2,1)S(1)} %copy-done.3, ...), custom_call_target="tpu_custom_call" | custom-call | flops 278921216 | bytes 4194304 | tf_op jit(solution)/shard_map/down_pieces_1/pallas_call | solution.py:232
  74.3 0.2 collective-permute-start.11
  74.5 1.9 %down_pieces_2.1 = (f32[4,224,512]{2,1,0:T(8,128)S(1)}, bf16[4,224,512]{2,1,0:T(8,128)(2,1)S(1)}) custom-call(s32[3]{0:T(128)S(1)} %pad_add_fusion.place, bf16[152,512]{1,0:T(8,128)(2,1)S(1)} %arrive_3_2.1.hidden, bf16[32,224,152]{2,1,0:T(8,128)(2,1)S(1)} %copy-done.2, bf16[32,224,152]{2,1,0:T(8,128)(2,1)S(1)} %copy-done.3, ...), custom_call_target="tpu_custom_call" | custom-call | flops 278921216 | bytes 4194304 | tf_op jit(solution)/shard_map/down_pieces_2/pallas_call | solution.py:232
  76.4 0.6 collective-permute-start.10
  77.1 0.0 collective-permute-done.11
  77.1 0.3 convert_add_fusion.1
  77.4 1.9 %down_pieces_3.1 = (f32[4,224,512]{2,1,0:T(8,128)S(1)}, bf16[4,224,512]{2,1,0:T(8,128)(2,1)S(1)}) custom-call(s32[3]{0:T(128)S(1)} %pad_add_fusion.place, bf16[152,512]{1,0:T(8,128)(2,1)S(1)} %arrive_3_2.1.hidden, bf16[32,224,152]{2,1,0:T(8,128)(2,1)S(1)} %copy-done.2, bf16[32,224,152]{2,1,0:T(8,128)(2,1)S(1)} %copy-done.3, ...), custom_call_target="tpu_custom_call" | custom-call | flops 278921216 | bytes 4194304 | tf_op jit(solution)/shard_map/down_pieces_3/pallas_call | solution.py:232
  79.3 0.2 collective-permute-start.15
  79.5 0.0 collective-permute-done.10
  79.5 0.3 convert_add_fusion.2
  79.8 1.9 %down_pieces_0.1 = (f32[4,224,512]{2,1,0:T(8,128)S(1)}, bf16[4,224,512]{2,1,0:T(8,128)(2,1)S(1)}) custom-call(s32[3]{0:T(128)S(1)} %pad_add_fusion.place, bf16[152,512]{1,0:T(8,128)(2,1)S(1)} %arrive_3_2.1.hidden, bf16[32,224,152]{2,1,0:T(8,128)(2,1)S(1)} %copy-done.2, bf16[32,224,152]{2,1,0:T(8,128)(2,1)S(1)} %copy-done.3, ...), custom_call_target="tpu_custom_call" | custom-call | flops 278921216 | bytes 4194304 | tf_op jit(solution)/shard_map/down_pieces_0/pallas_call | solution.py:232
  81.7 0.5 collective-permute-start.12
  82.2 0.9 collective-permute-start.14
  83.1 1.0 collective-permute-start.13
  84.1 0.3 add_convert_fusion
  84.4 1.5 %collective-permute-start.16 = (bf16[4,224,512]{2,1,0:T(8,128)(2,1)S(1)}, bf16[4,224,512]{2,1,0:T(8,128)(2,1)S(1)}, u32[]{:S(2)}, u32[]{:S(2)}) collective-permute-start(bf16[4,224,512]{2,1,0:T(8,128)(2,1)S(1)} %add_convert_fusion), channel_id=1, source_target_pairs={{0,6},{1,25},{2,0},{3,27},{4,2},{5,29},{6,4},{7,31},{8,14},{9,1},{... | collective-permute-start | bytes 2752520 | tf_op jit(solution)/shard_map/ppermute | solution.py:312
  86.0 11.2 %collective-permute-done.14 = bf16[4,224,512]{2,1,0:T(8,128)(2,1)S(1)} collective-permute-done((bf16[4,224,512]{2,1,0:T(8,128)(2,1)S(1)}, bf16[4,224,512]{2,1,0:T(8,128)(2,1)S(1)}, u32[]{:S(2)}, u32[]{:S(2)}) %collective-permute-start.14) | collective-permute-done | bytes 917536 | tf_op jit(solution)/shard_map/ppermute | solution.py:312
  97.2 9.6 %collective-permute-done.13 = bf16[4,224,512]{2,1,0:T(8,128)(2,1)S(1)} collective-permute-done((bf16[4,224,512]{2,1,0:T(8,128)(2,1)S(1)}, bf16[4,224,512]{2,1,0:T(8,128)(2,1)S(1)}, u32[]{:S(2)}, u32[]{:S(2)}) %collective-permute-start.13) | collective-permute-done | bytes 917536 | tf_op jit(solution)/shard_map/ppermute | solution.py:312
  106.8 0.1 collective-permute-done.16
  106.9 0.7 fusion.7
  107.7 1.0 collective-permute-start.17
  108.6 2.1 %collective-permute-start.18 = (bf16[224,512]{1,0:T(8,128)(2,1)S(1)}, bf16[224,512]{1,0:T(8,128)(2,1)S(1)}, u32[]{:S(2)}, u32[]{:S(2)}) collective-permute-start(bf16[224,512]{1,0:T(8,128)(2,1)S(1)} %get-tuple-element.97), channel_id=1, source_target_pairs={{0,16},{1,5},{2,18},{3,7},{4,20},{5,1},{6,22},{7,3},{8,24},{9,13},... | collective-permute-start | bytes 688136 | tf_op jit(solution)/shard_map/ppermute | solution.py:315
  110.7 1.6 %collective-permute-start.19 = (bf16[224,512]{1,0:T(8,128)(2,1)S(1)}, bf16[224,512]{1,0:T(8,128)(2,1)S(1)}, u32[]{:S(2)}, u32[]{:S(2)}) collective-permute-start(bf16[224,512]{1,0:T(8,128)(2,1)S(1)} %get-tuple-element.96), channel_id=1, source_target_pairs={{0,24},{1,7},{2,26},{3,1},{4,28},{5,3},{6,30},{7,5},{8,0},{9,15},{... | collective-permute-start | bytes 688136 | tf_op jit(solution)/shard_map/ppermute | solution.py:315
  112.3 5.1 %collective-permute-done.17 = bf16[224,512]{1,0:T(8,128)(2,1)S(1)} collective-permute-done((bf16[224,512]{1,0:T(8,128)(2,1)S(1)}, bf16[224,512]{1,0:T(8,128)(2,1)S(1)}, u32[]{:S(2)}, u32[]{:S(2)}) %collective-permute-start.17) | collective-permute-done | bytes 229408 | tf_op jit(solution)/shard_map/ppermute | solution.py:315
  117.4 0.0 collective-permute-done.18
  117.4 0.9 collective-permute-done.19
  118.3 0.1 fusion.2
  118.5 0.1 copy.13
  118.6 12.2 %all_to_all.11 = bf16[8,48,224]{2,1,0:T(8,128)(2,1)S(1)} all-to-all(bf16[8,48,224]{2,1,0:T(8,128)(2,1)S(1)} %bitcast.49), channel_id=1, replica_groups=mesh['expert'=8,'tensor'=32] {'expert'}, dimensions={0} | all-to-all | bytes 344064 | tf_op jit(solution)/shard_map/all_to_all | solution.py:318
  130.8 1.0 fusion.5
  (11 shorter events, 0.1 us)
Async XLA Ops:
  21.8 7.3 %collective-permute-start = (bf16[224,512]{1,0:T(8,128)(2,1)S(1)}, bf16[224,512]{1,0:T(8,128)(2,1)S(1)}, u32[]{:S(2)}, u32[]{:S(2)}) collective-permute-start(bf16[224,512]{1,0:T(8,128)(2,1)S(1)} %get-tuple-element.99), channel_id=1, source_target_pairs={{0,8},{1,3},{2,10},{3,5},{4,12},{5,7},{6,14},{7,1},{8,16},{9,11},{... | collective-permute-start | bytes 688136 | tf_op jit(solution)/shard_map/ppermute | solution.py:276
  23.4 9.2 %collective-permute-start.1 = (bf16[224,512]{1,0:T(8,128)(2,1)S(1)}, bf16[224,512]{1,0:T(8,128)(2,1)S(1)}, u32[]{:S(2)}, u32[]{:S(2)}) collective-permute-start(bf16[224,512]{1,0:T(8,128)(2,1)S(1)} %get-tuple-element.99), channel_id=1, source_target_pairs={{0,16},{1,5},{2,18},{3,7},{4,20},{5,1},{6,22},{7,3},{8,24},{9,13},... | collective-permute-start | bytes 688136 | tf_op jit(solution)/shard_map/ppermute | solution.py:276
  26.1 6.5 %collective-permute-start.2 = (bf16[224,512]{1,0:T(8,128)(2,1)S(1)}, bf16[224,512]{1,0:T(8,128)(2,1)S(1)}, u32[]{:S(2)}, u32[]{:S(2)}) collective-permute-start(bf16[224,512]{1,0:T(8,128)(2,1)S(1)} %get-tuple-element.99), channel_id=1, source_target_pairs={{0,24},{1,7},{2,26},{3,1},{4,28},{5,3},{6,30},{7,5},{8,0},{9,15},{... | collective-permute-start | bytes 688136 | tf_op jit(solution)/shard_map/ppermute | solution.py:276
  32.7 27.4 %collective-permute-start.5 = (bf16[4,224,512]{2,1,0:T(8,128)(2,1)S(1)}, bf16[4,224,512]{2,1,0:T(8,128)(2,1)}, u32[]{:S(2)}, u32[]{:S(2)}) collective-permute-start(bf16[4,224,512]{2,1,0:T(8,128)(2,1)S(1)} %pad_maximum_fusion.refs_0_), channel_id=1, source_target_pairs={{0,2},{1,9},{2,4},{3,11},{4,6},{5,13},{6,0},{7,15},{8,10},{9,17},{... | collective-permute-start | bytes 2752520 | tf_op jit(solution)/shard_map/ppermute | solution.py:278
  34.3 25.7 %collective-permute-start.6 = (bf16[4,224,512]{2,1,0:T(8,128)(2,1)S(1)}, bf16[4,224,512]{2,1,0:T(8,128)(2,1)}, u32[]{:S(2)}, u32[]{:S(2)}) collective-permute-start(bf16[4,224,512]{2,1,0:T(8,128)(2,1)S(1)} %pad_maximum_fusion.refs_0_), channel_id=1, source_target_pairs={{0,1},{1,0},{2,3},{3,2},{4,5},{5,4},{6,7},{7,6},{8,9},{9,8},{10,11... | collective-permute-start | bytes 2752520 | tf_op jit(solution)/shard_map/ppermute | solution.py:36
  34.3 31.0 %collective-permute-start.3 = (bf16[4,224,512]{2,1,0:T(8,128)(2,1)S(1)}, bf16[4,224,512]{2,1,0:T(8,128)(2,1)S(1)}, u32[]{:S(2)}, u32[]{:S(2)}) collective-permute-start(bf16[4,224,512]{2,1,0:T(8,128)(2,1)S(1)} %pad_maximum_fusion.refs_0_), channel_id=1, source_target_pairs={{0,4},{1,17},{2,6},{3,19},{4,0},{5,21},{6,2},{7,23},{8,12},{9,25},... | collective-permute-start | bytes 2752520 | tf_op jit(solution)/shard_map/ppermute | solution.py:278
  35.3 30.1 %collective-permute-start.4 = (bf16[4,224,512]{2,1,0:T(8,128)(2,1)S(1)}, bf16[4,224,512]{2,1,0:T(8,128)(2,1)S(1)}, u32[]{:S(2)}, u32[]{:S(2)}) collective-permute-start(bf16[4,224,512]{2,1,0:T(8,128)(2,1)S(1)} %pad_maximum_fusion.refs_0_), channel_id=1, source_target_pairs={{0,6},{1,25},{2,0},{3,27},{4,2},{5,29},{6,4},{7,31},{8,14},{9,1},{... | collective-permute-start | bytes 2752520 | tf_op jit(solution)/shard_map/ppermute | solution.py:278
  53.5 2.4 %copy-start = (bf16[32,304,224]{2,1,0:T(8,128)(2,1)S(1)}, bf16[32,304,224]{2,1,0:T(8,128)(2,1)}, u32[]{:S(2)}) copy-start(bf16[32,304,224]{2,1,0:T(8,128)(2,1)} %get-tuple-element.50.refs_1_.refs_2_.refs_3_.refs_4_.refs_5_) | copy-start | bytes 13074436
  55.9 2.4 %copy-start.1 = (bf16[32,304,224]{2,1,0:T(8,128)(2,1)S(1)}, bf16[32,304,224]{2,1,0:T(8,128)(2,1)}, u32[]{:S(2)}) copy-start(bf16[32,304,224]{2,1,0:T(8,128)(2,1)} %get-tuple-element.51.refs_2_.refs_4_.refs_5_.refs_6_.refs_7_.refs_8_) | copy-start | bytes 13074436
  60.1 5.9 %collective-permute-start.9 = (bf16[4,224,512]{2,1,0:T(8,128)(2,1)}, bf16[4,224,512]{2,1,0:T(8,128)(2,1)S(1)}, u32[]{:S(2)}, u32[]{:S(2)}) collective-permute-start(bf16[4,224,512]{2,1,0:T(8,128)(2,1)} %collective-permute-done.5.refs_1_), channel_id=1, source_target_pairs={{0,1},{1,0},{2,3},{3,2},{4,5},{5,4},{6,7},{7,6},{8,9},{9,8},{10,11... | collective-permute-start | bytes 2752520 | tf_op jit(solution)/shard_map/ppermute | solution.py:36
  65.4 3.5 %collective-permute-start.7 = (bf16[4,224,512]{2,1,0:T(8,128)(2,1)S(1)}, bf16[4,224,512]{2,1,0:T(8,128)(2,1)S(1)}, u32[]{:S(2)}, u32[]{:S(2)}) collective-permute-start(bf16[4,224,512]{2,1,0:T(8,128)(2,1)S(1)} %collective-permute-done.3.refs_1_), channel_id=1, source_target_pairs={{0,1},{1,0},{2,3},{3,2},{4,5},{5,4},{6,7},{7,6},{8,9},{9,8},{10,11... | collective-permute-start | bytes 2752520 | tf_op jit(solution)/shard_map/ppermute | solution.py:36
  65.5 3.8 %collective-permute-start.8 = (bf16[4,224,512]{2,1,0:T(8,128)(2,1)S(1)}, bf16[4,224,512]{2,1,0:T(8,128)(2,1)S(1)}, u32[]{:S(2)}, u32[]{:S(2)}) collective-permute-start(bf16[4,224,512]{2,1,0:T(8,128)(2,1)S(1)} %collective-permute-done.4.refs_2_), channel_id=1, source_target_pairs={{0,1},{1,0},{2,3},{3,2},{4,5},{5,4},{6,7},{7,6},{8,9},{9,8},{10,11... | collective-permute-start | bytes 2752520 | tf_op jit(solution)/shard_map/ppermute | solution.py:36
  69.3 2.5 %copy-start.2 = (bf16[32,224,152]{2,1,0:T(8,128)(2,1)S(1)}, bf16[32,224,152]{2,1,0:T(8,128)(2,1)}, u32[]{:S(2)}) copy-start(bf16[32,224,152]{2,1,0:T(8,128)(2,1)} %get-tuple-element.78.refs_0_.refs_2_) | copy-start | bytes 6537220
  69.3 3.2 %copy-start.3 = (bf16[32,224,152]{2,1,0:T(8,128)(2,1)S(1)}, bf16[32,224,152]{2,1,0:T(8,128)(2,1)}, u32[]{:S(2)}) copy-start(bf16[32,224,152]{2,1,0:T(8,128)(2,1)} %get-tuple-element.79.refs_1_.refs_3_) | copy-start | bytes 6537220
  74.3 2.8 %collective-permute-start.11 = (bf16[4,224,512]{2,1,0:T(8,128)(2,1)S(1)}, bf16[4,224,512]{2,1,0:T(8,128)(2,1)S(1)}, u32[]{:S(2)}, u32[]{:S(2)}) collective-permute-start(bf16[4,224,512]{2,1,0:T(8,128)(2,1)S(1)} %get-tuple-element.83), channel_id=1, source_target_pairs={{0,1},{1,0},{2,3},{3,2},{4,5},{5,4},{6,7},{7,6},{8,9},{9,8},{10,11... | collective-permute-start | bytes 2752520 | tf_op jit(solution)/shard_map/ppermute | solution.py:36
  76.4 3.1 %collective-permute-start.10 = (bf16[4,224,512]{2,1,0:T(8,128)(2,1)S(1)}, bf16[4,224,512]{2,1,0:T(8,128)(2,1)S(1)}, u32[]{:S(2)}, u32[]{:S(2)}) collective-permute-start(bf16[4,224,512]{2,1,0:T(8,128)(2,1)S(1)} %get-tuple-element.81), channel_id=1, source_target_pairs={{0,1},{1,0},{2,3},{3,2},{4,5},{5,4},{6,7},{7,6},{8,9},{9,8},{10,11... | collective-permute-start | bytes 2752520 | tf_op jit(solution)/shard_map/ppermute | solution.py:36
  79.3 4.8 %collective-permute-start.15 = (bf16[4,224,512]{2,1,0:T(8,128)(2,1)S(1)}, bf16[4,224,512]{2,1,0:T(8,128)(2,1)S(1)}, u32[]{:S(2)}, u32[]{:S(2)}) collective-permute-start(bf16[4,224,512]{2,1,0:T(8,128)(2,1)S(1)} %get-tuple-element.91), channel_id=1, source_target_pairs={{0,1},{1,0},{2,3},{3,2},{4,5},{5,4},{6,7},{7,6},{8,9},{9,8},{10,11... | collective-permute-start | bytes 2752520 | tf_op jit(solution)/shard_map/ppermute | solution.py:36
  81.7 4.2 %collective-permute-start.12 = (bf16[4,224,512]{2,1,0:T(8,128)(2,1)S(1)}, bf16[4,224,512]{2,1,0:T(8,128)(2,1)S(1)}, u32[]{:S(2)}, u32[]{:S(2)}) collective-permute-start(bf16[4,224,512]{2,1,0:T(8,128)(2,1)S(1)} %get-tuple-element.87), channel_id=1, source_target_pairs={{0,1},{1,0},{2,3},{3,2},{4,5},{5,4},{6,7},{7,6},{8,9},{9,8},{10,11... | collective-permute-start | bytes 2752520 | tf_op jit(solution)/shard_map/ppermute | solution.py:36
  82.2 15.0 %collective-permute-start.14 = (bf16[4,224,512]{2,1,0:T(8,128)(2,1)S(1)}, bf16[4,224,512]{2,1,0:T(8,128)(2,1)S(1)}, u32[]{:S(2)}, u32[]{:S(2)}) collective-permute-start(bf16[4,224,512]{2,1,0:T(8,128)(2,1)S(1)} %convert_add_fusion.2), channel_id=1, source_target_pairs={{0,4},{1,17},{2,6},{3,19},{4,0},{5,21},{6,2},{7,23},{8,12},{9,25},... | collective-permute-start | bytes 2752520 | tf_op jit(solution)/shard_map/ppermute | solution.py:312
  83.1 23.7 %collective-permute-start.13 = (bf16[4,224,512]{2,1,0:T(8,128)(2,1)S(1)}, bf16[4,224,512]{2,1,0:T(8,128)(2,1)S(1)}, u32[]{:S(2)}, u32[]{:S(2)}) collective-permute-start(bf16[4,224,512]{2,1,0:T(8,128)(2,1)S(1)} %convert_add_fusion.1), channel_id=1, source_target_pairs={{0,2},{1,9},{2,4},{3,11},{4,6},{5,13},{6,0},{7,15},{8,10},{9,17},{... | collective-permute-start | bytes 2752520 | tf_op jit(solution)/shard_map/ppermute | solution.py:312
  84.4 22.5 %collective-permute-start.16 = (bf16[4,224,512]{2,1,0:T(8,128)(2,1)S(1)}, bf16[4,224,512]{2,1,0:T(8,128)(2,1)S(1)}, u32[]{:S(2)}, u32[]{:S(2)}) collective-permute-start(bf16[4,224,512]{2,1,0:T(8,128)(2,1)S(1)} %add_convert_fusion), channel_id=1, source_target_pairs={{0,6},{1,25},{2,0},{3,27},{4,2},{5,29},{6,4},{7,31},{8,14},{9,1},{... | collective-permute-start | bytes 2752520 | tf_op jit(solution)/shard_map/ppermute | solution.py:312
  107.6 23.2 %copy-start.4 = (f32[384,128]{1,0:T(8,128)S(1)}, f32[384,128]{1,0:T(8,128)}, u32[]{:S(2)}) copy-start(f32[384,128]{1,0:T(8,128)} %get-tuple-element.92) | copy-start | bytes 589828
  107.7 9.8 %collective-permute-start.17 = (bf16[224,512]{1,0:T(8,128)(2,1)S(1)}, bf16[224,512]{1,0:T(8,128)(2,1)S(1)}, u32[]{:S(2)}, u32[]{:S(2)}) collective-permute-start(bf16[224,512]{1,0:T(8,128)(2,1)S(1)} %get-tuple-element.95), channel_id=1, source_target_pairs={{0,8},{1,3},{2,10},{3,5},{4,12},{5,7},{6,14},{7,1},{8,16},{9,11},{... | collective-permute-start | bytes 688136 | tf_op jit(solution)/shard_map/ppermute | solution.py:315
  108.6 8.8 %collective-permute-start.18 = (bf16[224,512]{1,0:T(8,128)(2,1)S(1)}, bf16[224,512]{1,0:T(8,128)(2,1)S(1)}, u32[]{:S(2)}, u32[]{:S(2)}) collective-permute-start(bf16[224,512]{1,0:T(8,128)(2,1)S(1)} %get-tuple-element.97), channel_id=1, source_target_pairs={{0,16},{1,5},{2,18},{3,7},{4,20},{5,1},{6,22},{7,3},{8,24},{9,13},... | collective-permute-start | bytes 688136 | tf_op jit(solution)/shard_map/ppermute | solution.py:315
  110.7 7.6 %collective-permute-start.19 = (bf16[224,512]{1,0:T(8,128)(2,1)S(1)}, bf16[224,512]{1,0:T(8,128)(2,1)S(1)}, u32[]{:S(2)}, u32[]{:S(2)}) collective-permute-start(bf16[224,512]{1,0:T(8,128)(2,1)S(1)} %get-tuple-element.96), channel_id=1, source_target_pairs={{0,24},{1,7},{2,26},{3,1},{4,28},{5,3},{6,30},{7,5},{8,0},{9,15},{... | collective-permute-start | bytes 688136 | tf_op jit(solution)/shard_map/ppermute | solution.py:315

commit v3 on v2

v3 whole, which is shorter than its diff:
```python
import functools

import jax
import jax.numpy as jnp
from jax import lax
from jax.experimental import pallas as pl
from jax.experimental.pallas import tpu as pltpu
from jax.sharding import PartitionSpec as P

SIDE = 4
PAIR = 2
CHIPS = SIDE * SIDE
GROUP = CHIPS * PAIR
F32 = jnp.float32
BF16 = jnp.bfloat16
MIB = 1024 * 1024
CHUNK = 896


def device_of(x, y, core):
    return (x * SIDE + y) * PAIR + core


def hops(step, first):
    pairs = []
    for x in range(SIDE):
        for y in range(SIDE):
            for core in range(PAIR):
                along_x = (core == 0) == first
                to_x = (x + step) % SIDE if along_x else x
                to_y = y if along_x else (y + step) % SIDE
                pairs.append((device_of(x, y, core), device_of(to_x, to_y, core)))
    return pairs


def sibling(value):
    return lax.ppermute(value, "tensor", [(i, i ^ 1) for i in range(GROUP)])


def piece_index(place, other, sign, outer, inner):
    x, y, core = place[0], place[1], place[2]
    owner = 1 - core if other else core
    move_x = jnp.where(owner == 0, inner, outer)
    move_y = jnp.where(owner == 0, outer, inner)
    at_x = lax.rem(x + sign * move_x + SIDE, SIDE)
    at_y = lax.rem(y + sign * move_y + SIDE, SIDE)
    return device_of(at_x, at_y, owner)


def dispatch_kernel(experts, capacity, ids, probs, tokens, outgoing, combine):
    choose, rows = ids.shape
    slots = experts * capacity
    numbers = lax.broadcasted_iota(jnp.int32, (experts, rows), 0)
    before = lax.broadcasted_iota(jnp.int32, (rows, rows), 0)
    after = lax.broadcasted_iota(jnp.int32, (rows, rows), 1)
    earlier = (before < after).astype(F32).astype(BF16)
    slot_numbers = lax.broadcasted_iota(jnp.int32, (slots, rows), 0)
    taken = jnp.zeros((experts, 1), F32)
    weights = jnp.zeros((slots, rows), F32)
    chosen = jnp.zeros((slots, rows), F32)
    for k in range(choose):
        named = ids[k : k + 1, :]
        onehot = (numbers == named).astype(F32)
        ahead = jnp.dot(onehot.astype(BF16), earlier, preferred_element_type=F32) + taken
        position = jnp.sum(ahead * onehot, axis=0, keepdims=True).astype(jnp.int32)
        hits = slot_numbers == named * capacity + position
        weights = weights + jnp.where(hits, probs[k : k + 1, :], 0.0)
        chosen = chosen + hits.astype(F32)
        taken = taken + jnp.sum(onehot, axis=1, keepdims=True)
    combine[...] = weights
    outgoing[...] = lax.dot_general(
        chosen.astype(BF16), tokens[...], (((1,), (1,)), ((), ())), preferred_element_type=F32
    ).astype(BF16)


def dispatched(ids, probs, tokens, experts, capacity):
    cols, rows = tokens.shape
    return pl.pallas_call(
        functools.partial(dispatch_kernel, experts, capacity),
        out_shape=(
            jax.ShapeDtypeStruct((experts * capacity, cols), BF16),
            jax.ShapeDtypeStruct((experts * capacity, rows), F32),
        ),
        name="dispatch",
    )(ids, probs, tokens)


def fetches(sources, targets, arrived):
    steps = sources[0].shape[1] // CHUNK
    copies = []
    for step in range(steps):
        at = slice(step * CHUNK, (step + 1) * CHUNK)
        copies.append(
            [
                pltpu.make_async_copy(source.at[:, at], target.at[:, at], arrived.at[i, step])
                for i, (source, target) in enumerate(zip(sources, targets))
            ]
        )
    for row in copies:
        for copy in row:
            copy.start()
    return copies


def fetched(count, units, width):
    return [pltpu.VMEM((units, width), BF16)] * count + [
        pltpu.SemaphoreType.DMA((count, width // CHUNK))
    ]


IN_HBM = pl.BlockSpec(memory_space=pltpu.MemorySpace.HBM)
IN_VMEM = pl.BlockSpec(memory_space=pltpu.MemorySpace.VMEM)


def up_weights_kernel(cols, gain, gate_source, up_source, out, gate, up, arrived):
    each = CHUNK // cols
    for step, copies in enumerate(fetches([gate_source, up_source], [gate, up], arrived)):
        for copy in copies:
            copy.wait()
        for i in range(step * each, (step + 1) * each):
            at = slice(i * cols, (i + 1) * cols)
            both = jnp.concatenate([gate[:, at].astype(F32), up[:, at].astype(F32)], axis=0)
            out[i] = (both * gain[:, at]).astype(BF16)


def up_weights(gain, gate, up, cols):
    units, width = gate.shape
    return pl.pallas_call(
        functools.partial(up_weights_kernel, cols),
        out_shape=jax.ShapeDtypeStruct((width // cols, 2 * units, cols), BF16),
        in_specs=[IN_VMEM, IN_HBM, IN_HBM],
        out_specs=IN_VMEM,
        scratch_shapes=fetched(2, units, width),
        compiler_params=pltpu.CompilerParams(vmem_limit_bytes=18 * MIB),
        cost_estimate=pl.CostEstimate(flops=MIB, bytes_accessed=MIB, transcendentals=0),
        name="up_weights",
    )(gain, gate, up)


def down_weights_kernel(cols, first_source, second_source, *refs):
    outs, scratch, arrived = refs[:2], refs[2:4], refs[4]
    each = CHUNK // cols
    for step, copies in enumerate(fetches([first_source, second_source], scratch, arrived)):
        for copy, weight, out in zip(copies, scratch, outs):
            copy.wait()
            for i in range(step * each, (step + 1) * each):
                out[i] = weight[:, i * cols : (i + 1) * cols].astype(F32).T.astype(BF16)


def down_weights(first, second, cols):
    units, width = first.shape
    shape = jax.ShapeDtypeStruct((width // cols, cols, units), BF16)
    return pl.pallas_call(
        functools.partial(down_weights_kernel, cols),
        out_shape=[shape, shape],
        in_specs=[IN_HBM, IN_HBM],
        out_specs=[IN_VMEM, IN_VMEM],
        scratch_shapes=fetched(2, units, width),
        compiler_params=pltpu.CompilerParams(vmem_limit_bytes=20 * MIB),
        cost_estimate=pl.CostEstimate(flops=MIB, bytes_accessed=MIB, transcendentals=0),
        name="down_weights",
    )(first, second)


def dense_kernel(gain, source, gate_source, up_source, hidden, gathered, gate, up, came, arrived):
    width, rows = gathered.shape
    rows_copy = pltpu.make_async_copy(source, gathered, came)
    rows_copy.start()
    copies = fetches([gate_source, up_source], [gate, up], arrived)
    rows_copy.wait()

    def squares(i, total):
        block = gathered[pl.ds(pl.multiple_of(i * CHUNK, CHUNK), CHUNK), :].astype(F32)
        block = block * block
        return total + jnp.sum(block.reshape(CHUNK // 8, 8, rows), axis=0)

    total = lax.fori_loop(0, width // CHUNK, squares, jnp.zeros((8, rows), F32))
    scale = lax.rsqrt(jnp.sum(total, axis=0, keepdims=True) / width + 1e-05)

    def product(weight, normed):
        return lax.dot_general(
            weight, normed, (((1,), (1,)), ((), ())), preferred_element_type=F32
        )

    gates = ups = jnp.zeros((gate.shape[0], rows), F32)
    for step, row in enumerate(copies):
        at = slice(step * CHUNK, (step + 1) * CHUNK)
        normed = ((gathered[at, :].astype(F32) * scale).T * gain[:, at]).astype(BF16)
        for copy in row:
            copy.wait()
        gates = gates + product(gate[:, at], normed)
        ups = ups + product(up[:, at], normed)
    hidden[...] = (gates / (1.0 + jnp.exp(-gates)) * ups).astype(BF16)


def dense_hidden_units(gathered, gain, gate, up):
    units, width = gate.shape
    rows = gathered.shape[1]
    return pl.pallas_call(
        dense_kernel,
        out_shape=jax.ShapeDtypeStruct((units, rows), BF16),
        in_specs=[IN_VMEM, IN_HBM, IN_HBM, IN_HBM],
        out_specs=IN_VMEM,
        scratch_shapes=[
            pltpu.VMEM((width, rows), BF16),
            pltpu.VMEM((units, width), BF16),
            pltpu.VMEM((units, width), BF16),
            pltpu.SemaphoreType.DMA,
            pltpu.SemaphoreType.DMA((2, width // CHUNK)),
        ],
        compiler_params=pltpu.CompilerParams(vmem_limit_bytes=14 * MIB),
        cost_estimate=pl.CostEstimate(flops=MIB, bytes_accessed=MIB, transcendentals=0),
        name="dense_hidden",
    )(gain, gathered, gate, up)


def arrive_kernel(count, start, last, width, place, *refs):
    stacks, weights, refs = refs[:count], refs[count : 2 * count], refs[2 * count :]
    if not start:
        carried, refs = refs[:2], refs[2:]
    if last:
        hidden, refs = refs[0], refs[1:]
    sums, squares = refs

    @pl.when(pl.program_id(0) == 0)
    def _():
        for i, ref in enumerate((sums, squares)):
            ref[...] = jnp.zeros_like(ref) if start else carried[i][...]

    for stack, weight in zip(stacks, weights):
        block = stack[0]
        sums[...] += jnp.dot(weight[0], block, preferred_element_type=F32)
        values = block.astype(F32)
        values = values * values
        squares[...] += jnp.sum(values.reshape(values.shape[0] // 8, 8, values.shape[1]), axis=0)

    if last:

        @pl.when(pl.program_id(0) == pl.num_programs(0) - 1)
        def _():
            scale = lax.rsqrt(jnp.sum(squares[...], axis=0, keepdims=True) / width + 1e-05)
            units = sums.shape[0] // 2
            gates, ups = sums[:units, :] * scale, sums[units:, :] * scale
            hidden[...] = (gates / (1.0 + jnp.exp(-gates)) * ups).astype(BF16)


def arrive(place, stage, weights, sums, last=False):
    count = len(stage)
    cols, rows = stage[0][0].shape[1:]
    height = weights.shape[1]
    start = sums is None

    def weight(outer, other):
        def index(i, place):
            return piece_index(place, other, -1, outer, i), 0, 0

        return pl.BlockSpec((1, height, cols), index)

    whole = lambda shape: pl.BlockSpec(shape, lambda i, place: (0, 0))
    shapes = [(height, rows), (8, rows)]
    sum_specs = [whole(s) for s in shapes]
    if last:
        out_specs = whole((height // 2, rows))
        out_shape = jax.ShapeDtypeStruct((height // 2, rows), BF16)
        scratch = [pltpu.VMEM(s, F32) for s in shapes]
    else:
        out_specs, scratch = sum_specs, []
        out_shape = [jax.ShapeDtypeStruct(s, F32) for s in shapes]
    return pl.pallas_call(
        functools.partial(arrive_kernel, count, start, last, GROUP * cols),
        out_shape=out_shape,
        grid_spec=pltpu.PrefetchScalarGridSpec(
            num_scalar_prefetch=1,
            grid=(SIDE,),
            in_specs=[pl.BlockSpec((1, cols, rows), lambda i, place: (i, 0, 0))] * count
            + [weight(outer, other) for _, outer, other in stage]
            + ([] if start else sum_specs),
            out_specs=out_specs,
            scratch_shapes=scratch,
        ),
        compiler_params=pltpu.CompilerParams(vmem_limit_bytes=8 * MIB),
        cost_estimate=pl.CostEstimate(flops=MIB, bytes_accessed=MIB, transcendentals=0),
        name=f"arrive_{stage[-1][1]}_{count}",
    )(
        place,
        *[stack for stack, _, _ in stage],
        *[weights] * count,
        *([] if start else sums),
    )


def down_kernel(place, hidden, weight, other_weight, mine, others):
    mine[0] = jnp.dot(weight[0], hidden[...], preferred_element_type=F32)
    others[0] = jnp.dot(other_weight[0], hidden[...], preferred_element_type=F32).astype(BF16)


def down_pieces(place, hidden, weights, first, steps):
    units, rows = hidden.shape
    cols = weights.shape[1]

    def weight(other):
        def index(i, place):
            return piece_index(place, other, 1, first + i // SIDE, i % SIDE), 0, 0

        return pl.BlockSpec((1, cols, units), index)

    out = pl.BlockSpec((1, cols, rows), lambda i, place: (i, 0, 0))
    shape = (steps * SIDE, cols, rows)
    return pl.pallas_call(
        down_kernel,
        out_shape=(jax.ShapeDtypeStruct(shape, F32), jax.ShapeDtypeStruct(shape, BF16)),
        grid_spec=pltpu.PrefetchScalarGridSpec(
            num_scalar_prefetch=1,
            grid=(steps * SIDE,),
            in_specs=[
                pl.BlockSpec((units, rows), lambda i, place: (0, 0)),
                weight(False),
                weight(True),
            ],
            out_specs=(out, out),
        ),
        compiler_params=pltpu.CompilerParams(vmem_limit_bytes=8 * MIB),
        cost_estimate=pl.CostEstimate(flops=MIB, bytes_accessed=MIB, transcendentals=0),
        name=f"down_pieces_{first}_{steps}",
    )(place, hidden, weights, weights)


def shards(
    tokens,
    norm_gain,
    route_ids,
    route_probs,
    dense_gate,
    dense_up,
    dense_down,
    expert_gate,
    expert_up,
    expert_down,
):
    experts = lax.axis_size("expert")
    rows, choose = route_ids.shape
    cols = tokens.shape[1]
    capacity = 3 * rows * choose // (2 * experts)
    index = lax.axis_index("tensor")
    place = jnp.stack([index // (SIDE * PAIR), index // PAIR % SIDE, index % PAIR]).astype(jnp.int32)

    gain = norm_gain[None, :]

    gathered = lax.all_gather(tokens.T, "tensor", axis=0, tiled=True)

    outgoing, combine = dispatched(route_ids.T, route_probs.T, tokens.T, experts, capacity)
    received = lax.all_to_all(
        outgoing.reshape(experts, capacity, cols), "expert", 0, 0, tiled=True
    ).reshape(experts * capacity, cols)
    own = received.T

    first = [own] + [lax.ppermute(own, "tensor", hops(d, True)) for d in range(1, SIDE)]
    stack = jnp.stack(first)
    near, far, left = [lax.ppermute(stack, "tensor", hops(d, False)) for d in (1, 2, 3)]
    stack_other = sibling(stack)
    weights = up_weights(gain, expert_gate[0], expert_up[0], cols)
    sums = arrive(place, [(stack, 0, False)], weights, None)
    near, stack_other, sums, expert_down = lax.optimization_barrier(
        (near, stack_other, sums, expert_down)
    )
    near_other = sibling(near)
    sums = arrive(place, [(stack_other, 0, True), (near, 1, False)], weights, sums)
    routed_down, dense_down = down_weights(expert_down[0], dense_down, cols)
    far, left, sums, routed_down, dense_down = lax.optimization_barrier(
        (far, left, sums, routed_down, dense_down)
    )
    far_other, left_other = sibling(far), sibling(left)
    sums = arrive(
        place, [(near_other, 1, True), (far, 2, False), (left, 3, False)], weights, sums
    )
    far_other, left_other, sums = lax.optimization_barrier((far_other, left_other, sums))
    hidden = arrive(
        place, [(far_other, 2, True), (left_other, 3, True)], weights, sums, last=True
    )

    hidden, gathered = lax.optimization_barrier((hidden, gathered))

    pieces = {}
    for outer in (1, 2, 3, 0):
        mine, others = down_pieces(place, hidden, routed_down, outer, 1)
        if outer > 1:
            pieces[outer - 1], hidden = lax.optimization_barrier((pieces[outer - 1], hidden))
        pieces[outer] = mine + sibling(others).astype(F32)
    leaving = [pieces[d].astype(BF16) for d in range(1, SIDE)]

    summed = [lax.ppermute(part, "tensor", hops(d, False)) for d, part in zip((1, 2, 3), leaving)]

    gathered, summed[0] = lax.optimization_barrier((gathered, summed[0]))
    dense_hidden = dense_hidden_units(gathered, gain, dense_gate, dense_up)
    mine, others = down_pieces(place, dense_hidden, dense_down, 0, SIDE)
    dense_pieces = (mine + sibling(others).astype(F32)).reshape(SIDE, SIDE, cols, rows)

    level = pieces[0]
    for part in summed:
        level = level + part.astype(F32)
    total = level[0]
    for d in range(1, SIDE):
        total = total + lax.ppermute(level[d].astype(BF16), "tensor", hops(d, True)).astype(F32)

    dense_level = dense_pieces[0]
    for d in range(1, SIDE):
        dense_level = dense_level + lax.ppermute(
            dense_pieces[d].astype(BF16), "tensor", hops(d, False)
        ).astype(F32)
    dense_total = dense_level[0]
    for d in range(1, SIDE):
        dense_total = dense_total + lax.ppermute(
            dense_level[d].astype(BF16), "tensor", hops(d, True)
        ).astype(F32)

    back = total.astype(BF16).T.reshape(experts, capacity, cols)
    returned = lax.all_to_all(back, "expert", 0, 0, tiled=True).reshape(experts * capacity, cols)
    moe_out = jnp.dot(combine.T, returned.astype(F32), precision=lax.Precision.HIGHEST)
    return (dense_total.T + moe_out).astype(BF16)


def solution(mesh):
    in_specs = (
        P("expert", "tensor"),
        P(),
        P("expert", None),
        P("expert", None),
        P("tensor", None),
        P("tensor", None),
        P("tensor", None),
        P("expert", "tensor", None),
        P("expert", "tensor", None),
        P("expert", "tensor", None),
    )
    out_specs = P("expert", "tensor")
    return jax.shard_map(shards, mesh=mesh, in_specs=in_specs, out_specs=out_specs, check_vma=False)
```

time: 133 us -> 144 us (1.083)
  the two profiles are of different devices: /device:TPU:8 before, /device:TPU:18 now
where the time goes in v3:
time: 144 us
  starting transfers between devices  43.1 us (30%)
  Pallas kernels  40 us (28%)
  waiting for transfers between devices  19.8 us (14%)
  blocking collectives  18.9 us (13%)
  between operations  13.8 us (10%)
  local copies, waits for them, and re-layouts  5.61 us (4%)
  other arithmetic  2.21 us (2%)
    all_to_all x1, blocking collectives, shards(): lax.all_to_all(outgoing.reshape(experts, capacity, cols), 'expert', 0, 0,...  18.9 us
    pallas_call x4, Pallas kernels, arrive(): pl.pallas_call(functools.partial(arrive_kernel, count, start, last, GROUP...  11.9 us
    pallas_call x5, Pallas kernels, down_pieces(): pl.pallas_call(down_kernel, out_shape=(jax.ShapeDtypeStruct(shape, F32),...  10.6 us
    all_to_all x1, starting transfers between devices, shards(): lax.all_to_all(back, 'expert', 0, 0, tiled=True)  9.43 us
    ppermute x3, starting transfers between devices, shards(): lax.ppermute(level[d].astype(BF16), 'tensor', hops(d, True)).astype(F32)  8.44 us
    pallas_call x1, Pallas kernels, down_weights(): pl.pallas_call(functools.partial(down_weights_kernel, cols), out_shape=[s...  7.6 us
    ppermute x3, waiting for transfers between devices, shards(): lax.ppermute(part, 'tensor', hops(d, False))  6.78 us
    ppermute x3, starting transfers between devices, shards(): lax.ppermute(dense_pieces[d].astype(BF16), 'tensor', hops(d, False))  6.25 us
  transfers between devices with their start and end apart: 29, of which 7 were waited for; matrix products, arithmetic and copies ran while one was open for 2% of the time, Pallas kernels for 27%

profile of v3, /device:TPU:18, one launch (start us, length us, event | category | flops | bytes accessed | tf_op | source)
XLA Modules:
  0.0 143.9 jit_solution(17433365004678554694)
XLA Ops:
  6.5 0.7 all-gather.2.cloned.1.call-update
  7.3 1.9 %dispatch.1 = (bf16[384,224]{1,0:T(8,128)(2,1)}, f32[384,128]{1,0:T(8,128)}) custom-call(s32[2,128]{1,0:T(2,128)} %bitcast.85, f32[2,128]{1,0:T(2,128)} %bitcast.86, bf16[224,128]{1,0:T(8,128)(2,1)} %bitcast.80), custom_call_target="tpu_custom_call" | custom-call | tf_op jit(solution)/shard_map/dispatch/pallas_call | solution.py:78
  9.1 18.9 %all_to_all.10 = bf16[8,48,224]{2,1,0:T(8,128)(2,1)S(1)} all-to-all(bf16[8,48,224]{2,1,0:T(8,128)(2,1)} %bitcast.81), channel_id=1, replica_groups=mesh['expert'=8,'tensor'=32] {'expert'}, dimensions={0} | all-to-all | bytes 344064 | tf_op jit(solution)/shard_map/all_to_all | solution.py:352
  28.1 0.1 copy.12
  28.2 1.6 %collective-permute-start = (bf16[224,384]{1,0:T(8,128)(2,1)S(1)}, bf16[224,384]{1,0:T(8,128)(2,1)S(1)}, u32[]{:S(2)}, u32[]{:S(2)}) collective-permute-start(bf16[224,384]{1,0:T(8,128)(2,1)S(1)} %bitcast.75), channel_id=1, source_target_pairs={{0,8},{1,3},{2,10},{3,5},{4,12},{5,7},{6,14},{7,1},{8,16},{9,11},{... | collective-permute-start | bytes 516104 | tf_op jit(solution)/shard_map/ppermute | solution.py:357
  29.8 1.1 collective-permute-start.1
  30.9 2.2 %collective-permute-start.2 = (bf16[224,384]{1,0:T(8,128)(2,1)S(1)}, bf16[224,384]{1,0:T(8,128)(2,1)S(1)}, u32[]{:S(2)}, u32[]{:S(2)}) collective-permute-start(bf16[224,384]{1,0:T(8,128)(2,1)S(1)} %bitcast.77), channel_id=1, source_target_pairs={{0,24},{1,7},{2,26},{3,1},{4,28},{5,3},{6,30},{7,5},{8,0},{9,15},{... | collective-permute-start | bytes 516104 | tf_op jit(solution)/shard_map/ppermute | solution.py:357
  33.1 0.9 collective-permute-done
  34.0 2.9 %collective-permute-done.1 = bf16[224,384]{1,0:T(8,128)(2,1)S(1)} collective-permute-done((bf16[224,384]{1,0:T(8,128)(2,1)S(1)}, bf16[224,384]{1,0:T(8,128)(2,1)S(1)}, u32[]{:S(2)}, u32[]{:S(2)}) %collective-permute-start.1) | collective-permute-done | bytes 172064 | tf_op jit(solution)/shard_map/ppermute | solution.py:357
  36.9 1.3 collective-permute-done.2
  38.2 0.1 pad_maximum_fusion.refs_0_
  38.3 1.4 collective-permute-start.5
  39.7 0.6 collective-permute-start.3
  40.4 1.1 collective-permute-start.4
  41.5 1.6 %copy-done.6 = bf16[1,152,7168]{2,1,0:T(8,128)(2,1)S(1)} copy-done((bf16[1,152,7168]{2,1,0:T(8,128)(2,1)S(1)}, bf16[1,152,7168]{2,1,0:T(8,128)(2,1)}, u32[]{:S(2)}) %copy-start.6) | copy-done | bytes 2179096
  43.1 0.7 copy-done.12
  43.8 3.3 %up_weights.1.refs_1_.refs_2_.refs_3_.refs_4_.refs_5_ = bf16[32,304,224]{2,1,0:T(8,128)(2,1)S(1)} custom-call(f32[1,7168]{1,0:T(1,128)S(1)} %bitcast.71, bf16[152,7168]{1,0:T(8,128)(2,1)S(1)} %bitcast.68, bf16[152,7168]{1,0:T(8,128)(2,1)S(1)} %bitcast.69), custom_call_target="tpu_custom_call" | custom-call | flops 1048576 | bytes 1048576 | tf_op jit(solution)/shard_map/up_weights/pallas_call | solution.py:128
  47.2 0.1 pad_add_fusion.place
  47.2 1.6 %arrive_0_1.1 = (f32[304,384]{1,0:T(8,128)S(1)}, f32[8,384]{1,0:T(8,128)S(1)}) custom-call(s32[3]{0:T(128)S(1)} %pad_add_fusion.place, bf16[4,224,384]{2,1,0:T(8,128)(2,1)S(1)} %pad_maximum_fusion.refs_0_, bf16[32,304,224]{2,1,0:T(8,128)(2,1)S(1)} %up_weights.1.refs_1_.refs_2_.refs_3_.refs_4_.refs_5_), custom_call_target="tpu_custom_call" | custom-call | flops 1048576 | bytes 1048576 | tf_op jit(solution)/shard_map/arrive_0_1/pallas_call | solution.py:269
  48.8 1.6 %collective-permute-done.5.refs_1_ = bf16[4,224,384]{2,1,0:T(8,128)(2,1)} collective-permute-done((bf16[4,224,384]{2,1,0:T(8,128)(2,1)S(1)}, bf16[4,224,384]{2,1,0:T(8,128)(2,1)}, u32[]{:S(2)}, u32[]{:S(2)}) %collective-permute-start.5) | collective-permute-done | bytes 688160 | tf_op jit(solution)/shard_map/ppermute | solution.py:359
  50.5 7.6 %down_weights.1 = (bf16[32,224,152]{2,1,0:T(8,128)(2,1)S(1)}, bf16[32,224,152]{2,1,0:T(8,128)(2,1)S(1)}) custom-call(bf16[152,7168]{1,0:T(8,128)(2,1)S(1)} %bitcast.70, bf16[152,7168]{1,0:T(8,128)(2,1)S(1)} %copy-done.8), custom_call_target="tpu_custom_call" | custom-call | flops 1048576 | bytes 1048576 | tf_op jit(solution)/shard_map/down_weights/pallas_call | solution.py:153
  58.1 4.5 %arrive_1_2.1 = (f32[304,384]{1,0:T(8,128)S(1)}, f32[8,384]{1,0:T(8,128)S(1)}) custom-call(s32[3]{0:T(128)S(1)} %pad_add_fusion.place, bf16[4,224,384]{2,1,0:T(8,128)(2,1)} %collective-permute-done.6.refs_0_, bf16[4,224,384]{2,1,0:T(8,128)(2,1)} %collective-permute-done.5.refs_1_, ...), custom_call_target="tpu_custom_call" | custom-call | flops 1048576 | bytes 1048576 | tf_op jit(solution)/shard_map/arrive_1_2/pallas_call | solution.py:269
  62.6 0.6 collective-permute-start.7
  63.2 0.1 collective-permute-start.8
  63.3 3.7 %arrive_3_3.1 = (f32[304,384]{1,0:T(8,128)S(1)}, f32[8,384]{1,0:T(8,128)S(1)}) custom-call(s32[3]{0:T(128)S(1)} %pad_add_fusion.place, bf16[4,224,384]{2,1,0:T(8,128)(2,1)S(1)} %collective-permute-done.9.refs_0_, bf16[4,224,384]{2,1,0:T(8,128)(2,1)S(1)} %collective-permute-done.3.refs_1_, bf16[4,224,384]{2,1,0:T(8,128)(2,1)} %collective-permute-done.4.refs_2_, ...), custom_call_target="tpu_custom_call" | custom-call | flops 1048576 | bytes 1048576 | tf_op jit(solution)/shard_map/arrive_3_3/pallas_call | solution.py:269
  67.1 2.1 %arrive_3_2.1.hidden = bf16[152,384]{1,0:T(8,128)(2,1)S(1)} custom-call(s32[3]{0:T(128)S(1)} %pad_add_fusion.place, bf16[4,224,384]{2,1,0:T(8,128)(2,1)S(1)} %collective-permute-done.7.refs_0_, bf16[4,224,384]{2,1,0:T(8,128)(2,1)S(1)} %collective-permute-done.8.refs_1_, bf16[32,304,224]{2,1,0:T(8,128)(2,1)S(1)} %up_weights.1.refs_1_.refs_2_.refs_3_.refs_4_.refs_5_, ...), custom_call_target="tpu_custom_call" | custom-call | flops 1048576 | bytes 1048576 | tf_op jit(solution)/shard_map/arrive_3_2/pallas_call | solution.py:269
  69.2 2.0 %copy-done.1 = bf16[32,224,152]{2,1,0:T(8,128)(2,1)S(1)} copy-done((bf16[32,224,152]{2,1,0:T(8,128)(2,1)S(1)}, bf16[32,224,152]{2,1,0:T(8,128)(2,1)}, u32[]{:S(2)}) %copy-start.1) | copy-done | bytes 2179096
  71.2 1.6 %down_pieces_1_1.1 = (f32[4,224,384]{2,1,0:T(8,128)S(1)}, bf16[4,224,384]{2,1,0:T(8,128)(2,1)S(1)}) custom-call(s32[3]{0:T(128)S(1)} %pad_add_fusion.place, bf16[152,384]{1,0:T(8,128)(2,1)S(1)} %arrive_3_2.1.hidden, bf16[32,224,152]{2,1,0:T(8,128)(2,1)S(1)} %copy-done.1, bf16[32,224,152]{2,1,0:T(8,128)(2,1)S(1)} %copy-done.1), custom_call_target="tpu_custom_call" | custom-call | flops 1048576 | bytes 1048576 | tf_op jit(solution)/shard_map/down_pieces_1_1/pallas_call | solution.py:309
  72.9 0.5 collective-permute-start.10
  73.4 1.6 %down_pieces_2_1.1 = (f32[4,224,384]{2,1,0:T(8,128)S(1)}, bf16[4,224,384]{2,1,0:T(8,128)(2,1)S(1)}) custom-call(s32[3]{0:T(128)S(1)} %pad_add_fusion.place, bf16[152,384]{1,0:T(8,128)(2,1)S(1)} %arrive_3_2.1.hidden, bf16[32,224,152]{2,1,0:T(8,128)(2,1)S(1)} %copy-done.1, bf16[32,224,152]{2,1,0:T(8,128)(2,1)S(1)} %copy-done.1), custom_call_target="tpu_custom_call" | custom-call | flops 1048576 | bytes 1048576 | tf_op jit(solution)/shard_map/down_pieces_2_1/pallas_call | solution.py:309
  75.1 0.2 collective-permute-start.19
  75.2 0.1 convert_add_fusion.3
  75.4 0.1 copy-done.2
  75.5 1.6 %down_pieces_3_1.1 = (f32[4,224,384]{2,1,0:T(8,128)S(1)}, bf16[4,224,384]{2,1,0:T(8,128)(2,1)S(1)}) custom-call(s32[3]{0:T(128)S(1)} %pad_add_fusion.place, bf16[152,384]{1,0:T(8,128)(2,1)S(1)} %arrive_3_2.1.hidden, bf16[32,224,152]{2,1,0:T(8,128)(2,1)S(1)} %copy-done.2, bf16[32,224,152]{2,1,0:T(8,128)(2,1)S(1)} %copy-done.2), custom_call_target="tpu_custom_call" | custom-call | flops 1048576 | bytes 1048576 | tf_op jit(solution)/shard_map/down_pieces_3_1/pallas_call | solution.py:309
  77.1 0.5 collective-permute-start.22
  77.6 0.9 collective-permute-start.11
  78.5 0.1 convert_add_fusion.2
  78.7 1.6 %down_pieces_0_1.1 = (f32[4,224,384]{2,1,0:T(8,128)S(1)}, bf16[4,224,384]{2,1,0:T(8,128)(2,1)S(1)}) custom-call(s32[3]{0:T(128)S(1)} %pad_add_fusion.place, bf16[152,384]{1,0:T(8,128)(2,1)S(1)} %arrive_3_2.1.hidden, bf16[32,224,152]{2,1,0:T(8,128)(2,1)S(1)} %copy-done.2, bf16[32,224,152]{2,1,0:T(8,128)(2,1)S(1)} %copy-done.2), custom_call_target="tpu_custom_call" | custom-call | flops 1048576 | bytes 1048576 | tf_op jit(solution)/shard_map/down_pieces_0_1/pallas_call | solution.py:309
  80.3 0.1 collective-permute-start.20
  80.4 2.0 %collective-permute-start.21 = (bf16[4,224,384]{2,1,0:T(8,128)(2,1)S(1)}, bf16[4,224,384]{2,1,0:T(8,128)(2,1)S(1)}, u32[]{:S(2)}, u32[]{:S(2)}) collective-permute-start(bf16[4,224,384]{2,1,0:T(8,128)(2,1)S(1)} %convert_add_fusion.2), channel_id=1, source_target_pairs={{0,4},{1,17},{2,6},{3,19},{4,0},{5,21},{6,2},{7,23},{8,12},{9,25},... | collective-permute-start | bytes 2064392 | tf_op jit(solution)/shard_map/ppermute | solution.py:391
  82.4 0.1 add_convert_fusion
  82.5 2.0 %collective-permute-start.23 = (bf16[4,224,384]{2,1,0:T(8,128)(2,1)S(1)}, bf16[4,224,384]{2,1,0:T(8,128)(2,1)S(1)}, u32[]{:S(2)}, u32[]{:S(2)}) collective-permute-start(bf16[4,224,384]{2,1,0:T(8,128)(2,1)S(1)} %add_convert_fusion), channel_id=1, source_target_pairs={{0,6},{1,25},{2,0},{3,27},{4,2},{5,29},{6,4},{7,31},{8,14},{9,1},{... | collective-permute-start | bytes 2064392 | tf_op jit(solution)/shard_map/ppermute | solution.py:391
  84.5 4.0 %collective-permute-done.11 = bf16[4,224,384]{2,1,0:T(8,128)(2,1)S(1)} collective-permute-done((bf16[4,224,384]{2,1,0:T(8,128)(2,1)S(1)}, bf16[4,224,384]{2,1,0:T(8,128)(2,1)S(1)}, u32[]{:S(2)}, u32[]{:S(2)}) %collective-permute-start.11) | collective-permute-done | bytes 688160 | tf_op jit(solution)/shard_map/ppermute | solution.py:391
  88.5 4.8 %dense_hidden.1.hidden = bf16[152,128]{1,0:T(8,128)(2,1)S(1)} custom-call(f32[1,7168]{1,0:T(1,128)S(1)} %bitcast.72, bf16[7168,128]{1,0:T(8,128)(2,1)S(1)} %copy-done.11, bf16[152,7168]{1,0:T(8,128)(2,1)S(1)} %copy-done.9, bf16[152,7168]{1,0:T(8,128)(2,1)S(1)} %copy-done.10), custom_call_target="tpu_custom_call" | custom-call | flops 1048576 | bytes 1048576 | tf_op jit(solution)/shard_map/dense_hidden/pallas_call | solution.py:199
  93.3 4.0 %down_pieces_0_4.1 = (f32[16,224,128]{2,1,0:T(8,128)S(1)}, bf16[16,224,128]{2,1,0:T(8,128)(2,1)S(1)}) custom-call(s32[3]{0:T(128)S(1)} %pad_add_fusion.place, bf16[152,128]{1,0:T(8,128)(2,1)S(1)} %dense_hidden.1.hidden, bf16[32,224,152]{2,1,0:T(8,128)(2,1)S(1)} %copy-done.4, bf16[32,224,152]{2,1,0:T(8,128)(2,1)S(1)} %copy-done.4), custom_call_target="tpu_custom_call" | custom-call | flops 1048576 | bytes 1048576 | tf_op jit(solution)/shard_map/down_pieces_0_4/pallas_call | solution.py:309
  97.4 0.1 collective-permute-start.12
  97.5 2.8 %collective-permute-done.23 = bf16[4,224,384]{2,1,0:T(8,128)(2,1)S(1)} collective-permute-done((bf16[4,224,384]{2,1,0:T(8,128)(2,1)S(1)}, bf16[4,224,384]{2,1,0:T(8,128)(2,1)S(1)}, u32[]{:S(2)}, u32[]{:S(2)}) %collective-permute-start.23) | collective-permute-done | bytes 688160 | tf_op jit(solution)/shard_map/ppermute | solution.py:391
  100.2 0.4 fusion.16
  100.7 1.0 collective-permute-start.24
  101.8 7.4 %collective-permute-start.25 = (bf16[224,384]{1,0:T(8,128)(2,1)S(1)}, bf16[224,384]{1,0:T(8,128)(2,1)S(1)}, u32[]{:S(2)}, u32[]{:S(2)}) collective-permute-start(bf16[224,384]{1,0:T(8,128)(2,1)S(1)} %get-tuple-element.102), channel_id=1, source_target_pairs={{0,16},{1,5},{2,18},{3,7},{4,20},{5,1},{6,22},{7,3},{8,24},{9,13},... | collective-permute-start | bytes 516104 | tf_op jit(solution)/shard_map/ppermute | solution.py:403
  109.2 0.3 fusion.15
  109.5 1.1 collective-permute-start.13
  110.7 2.6 %collective-permute-start.14 = (bf16[4,224,128]{2,1,0:T(8,128)(2,1)S(1)}, bf16[4,224,128]{2,1,0:T(8,128)(2,1)S(1)}, u32[]{:S(2)}, u32[]{:S(2)}) collective-permute-start(bf16[4,224,128]{2,1,0:T(8,128)(2,1)S(1)} %get-tuple-element.99), channel_id=1, source_target_pairs={{0,4},{1,17},{2,6},{3,19},{4,0},{5,21},{6,2},{7,23},{8,12},{9,25},... | collective-permute-start | bytes 688136 | tf_op jit(solution)/shard_map/ppermute | solution.py:407
  113.3 2.5 %collective-permute-start.15 = (bf16[4,224,128]{2,1,0:T(8,128)(2,1)S(1)}, bf16[4,224,128]{2,1,0:T(8,128)(2,1)S(1)}, u32[]{:S(2)}, u32[]{:S(2)}) collective-permute-start(bf16[4,224,128]{2,1,0:T(8,128)(2,1)S(1)} %get-tuple-element.98), channel_id=1, source_target_pairs={{0,6},{1,25},{2,0},{3,27},{4,2},{5,29},{6,4},{7,31},{8,14},{9,1},{... | collective-permute-start | bytes 688136 | tf_op jit(solution)/shard_map/ppermute | solution.py:407
  115.8 0.1 fusion.6
  115.9 0.8 copy.13
  116.7 9.4 %all-to-all-start.1 = ((bf16[8,48,224]{2,1,0:T(8,128)(2,1)}), bf16[8,48,224]{2,1,0:T(8,128)(2,1)S(1)}, u32[]{:S(2)}, u32[]{:S(2)}) async-start(bf16[8,48,224]{2,1,0:T(8,128)(2,1)} %bitcast.27), calls=%async_computation.1 | async-start | bytes 393216 | tf_op jit(solution)/shard_map/all_to_all | solution.py:417
  126.2 0.1 fusion.13
  126.3 0.1 collective-permute-start.16
  126.4 1.6 %collective-permute-start.17 = (bf16[224,128]{1,0:T(8,128)(2,1)S(1)}, bf16[224,128]{1,0:T(8,128)(2,1)S(1)}, u32[]{:S(2)}, u32[]{:S(2)}) collective-permute-start(bf16[224,128]{1,0:T(8,128)(2,1)S(1)} %get-tuple-element.105), channel_id=1, source_target_pairs={{0,16},{1,5},{2,18},{3,7},{4,20},{5,1},{6,22},{7,3},{8,24},{9,13},... | collective-permute-start | bytes 172040 | tf_op jit(solution)/shard_map/ppermute | solution.py:412
  128.0 2.5 %collective-permute-start.18 = (bf16[224,128]{1,0:T(8,128)(2,1)S(1)}, bf16[224,128]{1,0:T(8,128)(2,1)S(1)}, u32[]{:S(2)}, u32[]{:S(2)}) collective-permute-start(bf16[224,128]{1,0:T(8,128)(2,1)S(1)} %get-tuple-element.104), channel_id=1, source_target_pairs={{0,24},{1,7},{2,26},{3,1},{4,28},{5,3},{6,30},{7,5},{8,0},{9,15},{... | collective-permute-start | bytes 172040 | tf_op jit(solution)/shard_map/ppermute | solution.py:412
  130.5 5.4 %all-to-all-done.1 = bf16[8,48,224]{2,1,0:T(8,128)(2,1)S(1)} async-done(((bf16[8,48,224]{2,1,0:T(8,128)(2,1)}), bf16[8,48,224]{2,1,0:T(8,128)(2,1)S(1)}, u32[]{:S(2)}, u32[]{:S(2)}) %all-to-all-start.1) | async-done | bytes 172064 | tf_op jit(solution)/shard_map/all_to_all | solution.py:417
  135.9 0.4 fusion.18
  136.3 0.7 fusion.12
  (55 shorter events, 0.3 us)
Async XLA Ops:
  6.5 34.9 %copy-start.5 = (bf16[1,152,7168]{2,1,0:T(8,128)(2,1)S(1)}, bf16[1,152,7168]{2,1,0:T(8,128)(2,1)}, u32[]{:S(2)}) copy-start(bf16[1,152,7168]{2,1,0:T(8,128)(2,1)} %param.17) | copy-start | bytes 6537220
  6.5 62.7 %all-gather.2.cloned.1.call-start = ((), (), s32[]{:S(2)}) async-start(), calls=%async_computation.2 | async-start | bytes 1892352 | tf_op jit(solution)/shard_map/all_gather | solution.py:349
  28.2 5.7 %collective-permute-start = (bf16[224,384]{1,0:T(8,128)(2,1)S(1)}, bf16[224,384]{1,0:T(8,128)(2,1)S(1)}, u32[]{:S(2)}, u32[]{:S(2)}) collective-permute-start(bf16[224,384]{1,0:T(8,128)(2,1)S(1)} %bitcast.75), channel_id=1, source_target_pairs={{0,8},{1,3},{2,10},{3,5},{4,12},{5,7},{6,14},{7,1},{8,16},{9,11},{... | collective-permute-start | bytes 516104 | tf_op jit(solution)/shard_map/ppermute | solution.py:357
  29.8 7.1 %collective-permute-start.1 = (bf16[224,384]{1,0:T(8,128)(2,1)S(1)}, bf16[224,384]{1,0:T(8,128)(2,1)S(1)}, u32[]{:S(2)}, u32[]{:S(2)}) collective-permute-start(bf16[224,384]{1,0:T(8,128)(2,1)S(1)} %bitcast.76), channel_id=1, source_target_pairs={{0,16},{1,5},{2,18},{3,7},{4,20},{5,1},{6,22},{7,3},{8,24},{9,13},... | collective-permute-start | bytes 516104 | tf_op jit(solution)/shard_map/ppermute | solution.py:357
  30.9 7.3 %collective-permute-start.2 = (bf16[224,384]{1,0:T(8,128)(2,1)S(1)}, bf16[224,384]{1,0:T(8,128)(2,1)S(1)}, u32[]{:S(2)}, u32[]{:S(2)}) collective-permute-start(bf16[224,384]{1,0:T(8,128)(2,1)S(1)} %bitcast.77), channel_id=1, source_target_pairs={{0,24},{1,7},{2,26},{3,1},{4,28},{5,3},{6,30},{7,5},{8,0},{9,15},{... | collective-permute-start | bytes 516104 | tf_op jit(solution)/shard_map/ppermute | solution.py:357
  38.3 12.1 %collective-permute-start.5 = (bf16[4,224,384]{2,1,0:T(8,128)(2,1)S(1)}, bf16[4,224,384]{2,1,0:T(8,128)(2,1)}, u32[]{:S(2)}, u32[]{:S(2)}) collective-permute-start(bf16[4,224,384]{2,1,0:T(8,128)(2,1)S(1)} %pad_maximum_fusion.refs_0_), channel_id=1, source_target_pairs={{0,2},{1,9},{2,4},{3,11},{4,6},{5,13},{6,0},{7,15},{8,10},{9,17},{... | collective-permute-start | bytes 2064392 | tf_op jit(solution)/shard_map/ppermute | solution.py:359
  39.7 10.7 %collective-permute-start.6 = (bf16[4,224,384]{2,1,0:T(8,128)(2,1)S(1)}, bf16[4,224,384]{2,1,0:T(8,128)(2,1)}, u32[]{:S(2)}, u32[]{:S(2)}) collective-permute-start(bf16[4,224,384]{2,1,0:T(8,128)(2,1)S(1)} %pad_maximum_fusion.refs_0_), channel_id=1, source_target_pairs={{0,1},{1,0},{2,3},{3,2},{4,5},{5,4},{6,7},{7,6},{8,9},{9,8},{10,11... | collective-permute-start | bytes 2064392 | tf_op jit(solution)/shard_map/ppermute | solution.py:37
  39.7 22.9 %collective-permute-start.3 = (bf16[4,224,384]{2,1,0:T(8,128)(2,1)S(1)}, bf16[4,224,384]{2,1,0:T(8,128)(2,1)S(1)}, u32[]{:S(2)}, u32[]{:S(2)}) collective-permute-start(bf16[4,224,384]{2,1,0:T(8,128)(2,1)S(1)} %pad_maximum_fusion.refs_0_), channel_id=1, source_target_pairs={{0,4},{1,17},{2,6},{3,19},{4,0},{5,21},{6,2},{7,23},{8,12},{9,25},... | collective-permute-start | bytes 2064392 | tf_op jit(solution)/shard_map/ppermute | solution.py:359
  40.4 22.3 %collective-permute-start.4 = (bf16[4,224,384]{2,1,0:T(8,128)(2,1)S(1)}, bf16[4,224,384]{2,1,0:T(8,128)(2,1)}, u32[]{:S(2)}, u32[]{:S(2)}) collective-permute-start(bf16[4,224,384]{2,1,0:T(8,128)(2,1)S(1)} %pad_maximum_fusion.refs_0_), channel_id=1, source_target_pairs={{0,6},{1,25},{2,0},{3,27},{4,2},{5,29},{6,4},{7,31},{8,14},{9,1},{... | collective-permute-start | bytes 2064392 | tf_op jit(solution)/shard_map/ppermute | solution.py:359
  41.5 1.6 %copy-start.6 = (bf16[1,152,7168]{2,1,0:T(8,128)(2,1)S(1)}, bf16[1,152,7168]{2,1,0:T(8,128)(2,1)}, u32[]{:S(2)}) copy-start(bf16[1,152,7168]{2,1,0:T(8,128)(2,1)} %param.18) | copy-start | bytes 6537220
  43.1 0.7 copy-start.12
  47.2 3.2 %copy-start.7 = (bf16[1,152,7168]{2,1,0:T(8,128)(2,1)S(1)}, bf16[1,152,7168]{2,1,0:T(8,128)(2,1)}, u32[]{:S(2)}) copy-start(bf16[1,152,7168]{2,1,0:T(8,128)(2,1)} %param.19) | copy-start | bytes 6537220
  47.2 3.2 %copy-start.8 = (bf16[152,7168]{1,0:T(8,128)(2,1)S(1)}, bf16[152,7168]{1,0:T(8,128)(2,1)}, u32[]{:S(2)}) copy-start(bf16[152,7168]{1,0:T(8,128)(2,1)} %second_source.1) | copy-start | bytes 6537220
  50.5 12.9 %collective-permute-start.9 = (bf16[4,224,384]{2,1,0:T(8,128)(2,1)}, bf16[4,224,384]{2,1,0:T(8,128)(2,1)S(1)}, u32[]{:S(2)}, u32[]{:S(2)}) collective-permute-start(bf16[4,224,384]{2,1,0:T(8,128)(2,1)} %collective-permute-done.5.refs_1_), channel_id=1, source_target_pairs={{0,1},{1,0},{2,3},{3,2},{4,5},{5,4},{6,7},{7,6},{8,9},{9,8},{10,11... | collective-permute-start | bytes 2064392 | tf_op jit(solution)/shard_map/ppermute | solution.py:37
  58.1 4.5 %copy-start = (bf16[32,224,152]{2,1,0:T(8,128)(2,1)}, bf16[32,224,152]{2,1,0:T(8,128)(2,1)S(1)}, u32[]{:S(2)}) copy-start(bf16[32,224,152]{2,1,0:T(8,128)(2,1)S(1)} %get-tuple-element.72.weight.other_weight) | copy-start | bytes 6537220
  58.1 4.5 %copy-start.3 = (bf16[32,224,152]{2,1,0:T(8,128)(2,1)}, bf16[32,224,152]{2,1,0:T(8,128)(2,1)S(1)}, u32[]{:S(2)}) copy-start(bf16[32,224,152]{2,1,0:T(8,128)(2,1)S(1)} %get-tuple-element.77.weight.other_weight) | copy-start | bytes 6537220
  62.6 4.4 %collective-permute-start.7 = (bf16[4,224,384]{2,1,0:T(8,128)(2,1)S(1)}, bf16[4,224,384]{2,1,0:T(8,128)(2,1)S(1)}, u32[]{:S(2)}, u32[]{:S(2)}) collective-permute-start(bf16[4,224,384]{2,1,0:T(8,128)(2,1)S(1)} %collective-permute-done.3.refs_1_), channel_id=1, source_target_pairs={{0,1},{1,0},{2,3},{3,2},{4,5},{5,4},{6,7},{7,6},{8,9},{9,8},{10,11... | collective-permute-start | bytes 2064392 | tf_op jit(solution)/shard_map/ppermute | solution.py:37
  63.2 3.9 %collective-permute-start.8 = (bf16[4,224,384]{2,1,0:T(8,128)(2,1)}, bf16[4,224,384]{2,1,0:T(8,128)(2,1)S(1)}, u32[]{:S(2)}, u32[]{:S(2)}) collective-permute-start(bf16[4,224,384]{2,1,0:T(8,128)(2,1)} %collective-permute-done.4.refs_2_), channel_id=1, source_target_pairs={{0,1},{1,0},{2,3},{3,2},{4,5},{5,4},{6,7},{7,6},{8,9},{9,8},{10,11... | collective-permute-start | bytes 2064392 | tf_op jit(solution)/shard_map/ppermute | solution.py:37
  69.2 2.0 %copy-start.1 = (bf16[32,224,152]{2,1,0:T(8,128)(2,1)S(1)}, bf16[32,224,152]{2,1,0:T(8,128)(2,1)}, u32[]{:S(2)}) copy-start(bf16[32,224,152]{2,1,0:T(8,128)(2,1)} %copy-done) | copy-start | bytes 6537220
  72.9 2.3 %collective-permute-start.10 = (bf16[4,224,384]{2,1,0:T(8,128)(2,1)S(1)}, bf16[4,224,384]{2,1,0:T(8,128)(2,1)S(1)}, u32[]{:S(2)}, u32[]{:S(2)}) collective-permute-start(bf16[4,224,384]{2,1,0:T(8,128)(2,1)S(1)} %get-tuple-element.74), channel_id=1, source_target_pairs={{0,1},{1,0},{2,3},{3,2},{4,5},{5,4},{6,7},{7,6},{8,9},{9,8},{10,11... | collective-permute-start | bytes 2064392 | tf_op jit(solution)/shard_map/ppermute | solution.py:37
  73.4 2.0 %copy-start.2 = (bf16[32,224,152]{2,1,0:T(8,128)(2,1)S(1)}, bf16[32,224,152]{2,1,0:T(8,128)(2,1)}, u32[]{:S(2)}) copy-start(bf16[32,224,152]{2,1,0:T(8,128)(2,1)} %copy-done) | copy-start | bytes 6537220
  75.1 3.4 %collective-permute-start.19 = (bf16[4,224,384]{2,1,0:T(8,128)(2,1)S(1)}, bf16[4,224,384]{2,1,0:T(8,128)(2,1)S(1)}, u32[]{:S(2)}, u32[]{:S(2)}) collective-permute-start(bf16[4,224,384]{2,1,0:T(8,128)(2,1)S(1)} %get-tuple-element.82), channel_id=1, source_target_pairs={{0,1},{1,0},{2,3},{3,2},{4,5},{5,4},{6,7},{7,6},{8,9},{9,8},{10,11... | collective-permute-start | bytes 2064392 | tf_op jit(solution)/shard_map/ppermute | solution.py:37
  77.1 5.3 %collective-permute-start.22 = (bf16[4,224,384]{2,1,0:T(8,128)(2,1)S(1)}, bf16[4,224,384]{2,1,0:T(8,128)(2,1)S(1)}, u32[]{:S(2)}, u32[]{:S(2)}) collective-permute-start(bf16[4,224,384]{2,1,0:T(8,128)(2,1)S(1)} %get-tuple-element.90), channel_id=1, source_target_pairs={{0,1},{1,0},{2,3},{3,2},{4,5},{5,4},{6,7},{7,6},{8,9},{9,8},{10,11... | collective-permute-start | bytes 2064392 | tf_op jit(solution)/shard_map/ppermute | solution.py:37
  77.6 10.9 %collective-permute-start.11 = (bf16[4,224,384]{2,1,0:T(8,128)(2,1)S(1)}, bf16[4,224,384]{2,1,0:T(8,128)(2,1)S(1)}, u32[]{:S(2)}, u32[]{:S(2)}) collective-permute-start(bf16[4,224,384]{2,1,0:T(8,128)(2,1)S(1)} %convert_add_fusion.3), channel_id=1, source_target_pairs={{0,2},{1,9},{2,4},{3,11},{4,6},{5,13},{6,0},{7,15},{8,10},{9,17},{... | collective-permute-start | bytes 2064392 | tf_op jit(solution)/shard_map/ppermute | solution.py:391
  78.6 9.9 %copy-start.10 = (bf16[152,7168]{1,0:T(8,128)(2,1)S(1)}, bf16[152,7168]{1,0:T(8,128)(2,1)}, u32[]{:S(2)}) copy-start(bf16[152,7168]{1,0:T(8,128)(2,1)} %up_source.1) | copy-start | bytes 6537220
  78.6 9.9 %copy-start.11 = (bf16[7168,128]{1,0:T(8,128)(2,1)S(1)}, bf16[7168,128]{1,0:T(8,128)(2,1)}, u32[]{:S(2)}) copy-start(bf16[7168,128]{1,0:T(8,128)(2,1)} %all-gather.2.cloned.1.call-done.source) | copy-start | bytes 5505028
  80.3 17.2 %collective-permute-start.20 = (bf16[4,224,384]{2,1,0:T(8,128)(2,1)S(1)}, bf16[4,224,384]{2,1,0:T(8,128)(2,1)S(1)}, u32[]{:S(2)}, u32[]{:S(2)}) collective-permute-start(bf16[4,224,384]{2,1,0:T(8,128)(2,1)S(1)} %get-tuple-element.86), channel_id=1, source_target_pairs={{0,1},{1,0},{2,3},{3,2},{4,5},{5,4},{6,7},{7,6},{8,9},{9,8},{10,11... | collective-permute-start | bytes 2064392 | tf_op jit(solution)/shard_map/ppermute | solution.py:37
  80.4 17.1 %collective-permute-start.21 = (bf16[4,224,384]{2,1,0:T(8,128)(2,1)S(1)}, bf16[4,224,384]{2,1,0:T(8,128)(2,1)S(1)}, u32[]{:S(2)}, u32[]{:S(2)}) collective-permute-start(bf16[4,224,384]{2,1,0:T(8,128)(2,1)S(1)} %convert_add_fusion.2), channel_id=1, source_target_pairs={{0,4},{1,17},{2,6},{3,19},{4,0},{5,21},{6,2},{7,23},{8,12},{9,25},... | collective-permute-start | bytes 2064392 | tf_op jit(solution)/shard_map/ppermute | solution.py:391
  82.4 6.2 %copy-start.9 = (bf16[152,7168]{1,0:T(8,128)(2,1)S(1)}, bf16[152,7168]{1,0:T(8,128)(2,1)}, u32[]{:S(2)}) copy-start(bf16[152,7168]{1,0:T(8,128)(2,1)} %gate_source.1) | copy-start | bytes 6537220
  82.4 6.2 %copy-start.13 = (f32[7168]{0:T(1024)S(1)}, f32[7168]{0:T(1024)}, u32[]{:S(2)}) copy-start(f32[7168]{0:T(1024)} %param.11) | copy-start | bytes 86020
  82.5 17.7 %collective-permute-start.23 = (bf16[4,224,384]{2,1,0:T(8,128)(2,1)S(1)}, bf16[4,224,384]{2,1,0:T(8,128)(2,1)S(1)}, u32[]{:S(2)}, u32[]{:S(2)}) collective-permute-start(bf16[4,224,384]{2,1,0:T(8,128)(2,1)S(1)} %add_convert_fusion), channel_id=1, source_target_pairs={{0,6},{1,25},{2,0},{3,27},{4,2},{5,29},{6,4},{7,31},{8,14},{9,1},{... | collective-permute-start | bytes 2064392 | tf_op jit(solution)/shard_map/ppermute | solution.py:391
  88.5 4.8 %copy-start.4 = (bf16[32,224,152]{2,1,0:T(8,128)(2,1)S(1)}, bf16[32,224,152]{2,1,0:T(8,128)(2,1)}, u32[]{:S(2)}) copy-start(bf16[32,224,152]{2,1,0:T(8,128)(2,1)} %copy-done.3) | copy-start | bytes 6537220
  97.4 11.8 %collective-permute-start.12 = (bf16[16,224,128]{2,1,0:T(8,128)(2,1)S(1)}, bf16[16,224,128]{2,1,0:T(8,128)(2,1)S(1)}, u32[]{:S(2)}, u32[]{:S(2)}) collective-permute-start(bf16[16,224,128]{2,1,0:T(8,128)(2,1)S(1)} %get-tuple-element.79), channel_id=1, source_target_pairs={{0,1},{1,0},{2,3},{3,2},{4,5},{5,4},{6,7},{7,6},{8,9},{9,8},{10,11... | collective-permute-start | bytes 2752520 | tf_op jit(solution)/shard_map/ppermute | solution.py:37
  100.7 12.5 %collective-permute-start.24 = (bf16[224,384]{1,0:T(8,128)(2,1)S(1)}, bf16[224,384]{1,0:T(8,128)(2,1)S(1)}, u32[]{:S(2)}, u32[]{:S(2)}) collective-permute-start(bf16[224,384]{1,0:T(8,128)(2,1)S(1)} %get-tuple-element.100), channel_id=1, source_target_pairs={{0,8},{1,3},{2,10},{3,5},{4,12},{5,7},{6,14},{7,1},{8,16},{9,11},{... | collective-permute-start | bytes 516104 | tf_op jit(solution)/shard_map/ppermute | solution.py:403
  101.8 14.0 %collective-permute-start.25 = (bf16[224,384]{1,0:T(8,128)(2,1)S(1)}, bf16[224,384]{1,0:T(8,128)(2,1)S(1)}, u32[]{:S(2)}, u32[]{:S(2)}) collective-permute-start(bf16[224,384]{1,0:T(8,128)(2,1)S(1)} %get-tuple-element.102), channel_id=1, source_target_pairs={{0,16},{1,5},{2,18},{3,7},{4,20},{5,1},{6,22},{7,3},{8,24},{9,13},... | collective-permute-start | bytes 516104 | tf_op jit(solution)/shard_map/ppermute | solution.py:403
  109.1 6.6 %collective-permute-start.26 = (bf16[224,384]{1,0:T(8,128)(2,1)S(1)}, bf16[224,384]{1,0:T(8,128)(2,1)S(1)}, u32[]{:S(2)}, u32[]{:S(2)}) collective-permute-start(bf16[224,384]{1,0:T(8,128)(2,1)S(1)} %get-tuple-element.101), channel_id=1, source_target_pairs={{0,24},{1,7},{2,26},{3,1},{4,28},{5,3},{6,30},{7,5},{8,0},{9,15},{... | collective-permute-start | bytes 516104 | tf_op jit(solution)/shard_map/ppermute | solution.py:403
  109.5 16.6 %collective-permute-start.13 = (bf16[4,224,128]{2,1,0:T(8,128)(2,1)S(1)}, bf16[4,224,128]{2,1,0:T(8,128)(2,1)S(1)}, u32[]{:S(2)}, u32[]{:S(2)}) collective-permute-start(bf16[4,224,128]{2,1,0:T(8,128)(2,1)S(1)} %get-tuple-element.97), channel_id=1, source_target_pairs={{0,2},{1,9},{2,4},{3,11},{4,6},{5,13},{6,0},{7,15},{8,10},{9,17},{... | collective-permute-start | bytes 688136 | tf_op jit(solution)/shard_map/ppermute | solution.py:407
  110.7 15.5 %collective-permute-start.14 = (bf16[4,224,128]{2,1,0:T(8,128)(2,1)S(1)}, bf16[4,224,128]{2,1,0:T(8,128)(2,1)S(1)}, u32[]{:S(2)}, u32[]{:S(2)}) collective-permute-start(bf16[4,224,128]{2,1,0:T(8,128)(2,1)S(1)} %get-tuple-element.99), channel_id=1, source_target_pairs={{0,4},{1,17},{2,6},{3,19},{4,0},{5,21},{6,2},{7,23},{8,12},{9,25},... | collective-permute-start | bytes 688136 | tf_op jit(solution)/shard_map/ppermute | solution.py:407
  113.3 12.9 %collective-permute-start.15 = (bf16[4,224,128]{2,1,0:T(8,128)(2,1)S(1)}, bf16[4,224,128]{2,1,0:T(8,128)(2,1)S(1)}, u32[]{:S(2)}, u32[]{:S(2)}) collective-permute-start(bf16[4,224,128]{2,1,0:T(8,128)(2,1)S(1)} %get-tuple-element.98), channel_id=1, source_target_pairs={{0,6},{1,25},{2,0},{3,27},{4,2},{5,29},{6,4},{7,31},{8,14},{9,1},{... | collective-permute-start | bytes 688136 | tf_op jit(solution)/shard_map/ppermute | solution.py:407
  116.7 19.2 %all-to-all-start.1 = ((bf16[8,48,224]{2,1,0:T(8,128)(2,1)}), bf16[8,48,224]{2,1,0:T(8,128)(2,1)S(1)}, u32[]{:S(2)}, u32[]{:S(2)}) async-start(bf16[8,48,224]{2,1,0:T(8,128)(2,1)} %bitcast.27), calls=%async_computation.1 | async-start | bytes 393216 | tf_op jit(solution)/shard_map/all_to_all | solution.py:417
  126.1 9.8 %copy-start.14 = (f32[384,128]{1,0:T(8,128)S(1)}, f32[384,128]{1,0:T(8,128)}, u32[]{:S(2)}) copy-start(f32[384,128]{1,0:T(8,128)} %get-tuple-element.80) | copy-start | bytes 589828
  126.3 10.0 %collective-permute-start.16 = (bf16[224,128]{1,0:T(8,128)(2,1)S(1)}, bf16[224,128]{1,0:T(8,128)(2,1)S(1)}, u32[]{:S(2)}, u32[]{:S(2)}) collective-permute-start(bf16[224,128]{1,0:T(8,128)(2,1)S(1)} %get-tuple-element.103), channel_id=1, source_target_pairs={{0,8},{1,3},{2,10},{3,5},{4,12},{5,7},{6,14},{7,1},{8,16},{9,11},{... | collective-permute-start | bytes 172040 | tf_op jit(solution)/shard_map/ppermute | solution.py:412
  126.4 9.9 %collective-permute-start.17 = (bf16[224,128]{1,0:T(8,128)(2,1)S(1)}, bf16[224,128]{1,0:T(8,128)(2,1)S(1)}, u32[]{:S(2)}, u32[]{:S(2)}) collective-permute-start(bf16[224,128]{1,0:T(8,128)(2,1)S(1)} %get-tuple-element.105), channel_id=1, source_target_pairs={{0,16},{1,5},{2,18},{3,7},{4,20},{5,1},{6,22},{7,3},{8,24},{9,13},... | collective-permute-start | bytes 172040 | tf_op jit(solution)/shard_map/ppermute | solution.py:412
  128.0 8.4 %collective-permute-start.18 = (bf16[224,128]{1,0:T(8,128)(2,1)S(1)}, bf16[224,128]{1,0:T(8,128)(2,1)S(1)}, u32[]{:S(2)}, u32[]{:S(2)}) collective-permute-start(bf16[224,128]{1,0:T(8,128)(2,1)S(1)} %get-tuple-element.104), channel_id=1, source_target_pairs={{0,24},{1,7},{2,26},{3,1},{4,28},{5,3},{6,30},{7,5},{8,0},{9,15},{... | collective-permute-start | bytes 172040 | tf_op jit(solution)/shard_map/ppermute | solution.py:412
Sparse Core Ops, SparseCore 0:
  9.9 53.3 all-gather.1
